TPU v7x, 32 devices: a whole 2x2x4 slice. The times are simulated.
32 devices in a mesh: dp: 8 (over z, y), tensor: 4 (over x, core).
Axes of the slice: x: 2, y: 2, z: 4, core: 2. Of those that a mesh axis runs over, the one named last changes fastest.
Arguments:
- tokens: bfloat16 [16384, 1536], P(('dp', 'tensor')), may hold values from -6 to 6
- w_query: bfloat16 [1536, 1536], P('dp', 'tensor'), may hold values from -0.15625 to 0.15625
- w_keyval: bfloat16 [1536, 256], P('dp'), may hold values from -0.15625 to 0.15625
- w_out: bfloat16 [1536, 1536], P('tensor', 'dp'), may hold values from -0.625 to 0.625
- w_gate: bfloat16 [1536, 4608], P('dp', 'tensor'), may hold values from -0.15625 to 0.15625
- w_up: bfloat16 [1536, 4608], P('dp', 'tensor'), may hold values from -0.15625 to 0.15625
- w_down: bfloat16 [4608, 1536], P('tensor', 'dp'), may hold values from -0.09375 to 0.09375
- norm_gains: bfloat16 [2, 1536], P(None, 'dp'), may hold values from 0.25 to 1.75
- segment_ids: int32 [16384], P('dp'), may hold values from 0 to 2048, as said below
- grad_output: float32 [16384, 1536], P(('dp', 'tensor')), may hold values from -6 to 6
Outputs:
- output: bfloat16 [16384, 1536], P(('dp', 'tensor'))
- grad_tokens: float32 [16384, 1536], P(('dp', 'tensor'))
- grad_w_query: float32 [1536, 1536], P('dp', 'tensor')
- grad_w_keyval: float32 [1536, 256], P('dp')
- grad_w_out: float32 [1536, 1536], P('tensor', 'dp')
- grad_w_gate: float32 [1536, 4608], P('dp', 'tensor')
- grad_w_up: float32 [1536, 4608], P('dp', 'tensor')
- grad_w_down: float32 [4608, 1536], P('tensor', 'dp')
- grad_norm_gains: float32 [2, 1536], P(None, 'dp')
Inputs may be any that keep to these rules, and one draw needn't show every extreme that they name: `segment_ids`: within each sequence of 2048 tokens the ids never fall except to 0; 0 marks padding, which only ends a sequence; a change of id starts a new document; the last document of every sequence has id 2048.
All inputs are finite; a program needn't handle non-finite values.
Results may differ from a plain program's by a relative error of at most 0.014.
Values may be sent and summed in bfloat16 or wider, within the bound.
A program may use at most 192 MiB of HBM per device.

v0:
```python
import jax
import jax.numpy as jnp
from jax import lax
from jax.sharding import PartitionSpec as P

WINDOW = 1024


norm_epsilon = 1e-06
masked_score = -1e30


def rms_scaled(rows_in, gain_row):
    mean_square = jnp.mean(rows_in * rows_in, axis=-1, keepdims=True)
    return rows_in * lax.rsqrt(mean_square + norm_epsilon) * gain_row


def gated_gelu(gate_act, up_act):
    return jax.nn.gelu(gate_act, approximate=True) * up_act


def positions_of(segments):
    places = jnp.arange(segments.shape[0], dtype=jnp.int32)
    previous = jnp.concatenate([jnp.full((1,), -1, jnp.int32), segments[:-1]])
    starts = lax.cummax(jnp.where(segments != previous, places, 0), axis=0)
    return (places - starts).astype(jnp.float32)


def rotary_tables(positions, head_dim):
    half_dim = head_dim // 2
    inverse = 10000.0 ** (-jnp.arange(half_dim, dtype=jnp.float32) / half_dim)
    angles = positions[:, None] * inverse[None, :]
    return (jnp.cos(angles), jnp.sin(angles))


def rotary(vectors, cosine_table, sine_table):
    half_dim = vectors.shape[-1] // 2
    first_half = vectors[..., :half_dim]
    second_half = vectors[..., half_dim:]
    return jnp.concatenate(
        [
            first_half * cosine_table - second_half * sine_table,
            second_half * cosine_table + first_half * sine_table,
        ],
        axis=-1,
    )


def contract_last(left, right):
    return lax.dot_general(
        left, right, (((1,), (1,)), ((), ())), preferred_element_type=jnp.float32
    )


def contract_first(left, right):
    return lax.dot_general(
        left, right, (((0,), (0,)), ((), ())), preferred_element_type=jnp.float32
    )


def block_mask(segments, pad_segments, first_row, block_rows):
    seg_q = lax.dynamic_slice_in_dim(segments, first_row, block_rows, 0)
    seg_k = lax.dynamic_slice_in_dim(pad_segments, first_row, block_rows + WINDOW, 0)
    q_pos = first_row + jnp.arange(block_rows, dtype=jnp.int32)
    k_pos = first_row - WINDOW + jnp.arange(block_rows + WINDOW, dtype=jnp.int32)
    row_gap = q_pos[:, None] - k_pos[None, :]
    return (row_gap >= 0) & (row_gap < WINDOW) & (seg_q[:, None] == seg_k[None, :])


def block_scores(queries, pad_keys, segments, pad_segments, first_row, block_rows):
    score_scale = queries.shape[2] ** (-0.5)
    q_blk = lax.dynamic_slice_in_dim(queries, first_row, block_rows, 0)
    k_blk = lax.dynamic_slice_in_dim(pad_keys, first_row, block_rows + WINDOW, 0)
    allowed = block_mask(segments, pad_segments, first_row, block_rows)
    scores = (
        jnp.einsum("qhd,kd->hqk", q_blk, k_blk, preferred_element_type=jnp.float32) * score_scale
    )
    return (q_blk, k_blk, jnp.where(allowed[None], scores, masked_score))


def attention_forward(queries, pad_keys, pad_values, segments, pad_segments):
    length_now, group_heads, head_dim = queries.shape
    block_rows = min(512, length_now)

    def one_block(block_step, running):
        attended, log_totals = running
        first_row = block_step * block_rows
        q_blk, k_blk, scores = block_scores(
            queries, pad_keys, segments, pad_segments, first_row, block_rows
        )
        v_blk = lax.dynamic_slice_in_dim(pad_values, first_row, block_rows + WINDOW, 0)
        row_peak = jnp.max(scores, axis=-1, keepdims=True)
        exp_scores = jnp.exp(scores - row_peak)
        denominator = jnp.sum(exp_scores, axis=-1, keepdims=True)
        block_probs = (exp_scores / denominator).astype(jnp.bfloat16)
        o_blk = jnp.einsum("hqk,kd->qhd", block_probs, v_blk, preferred_element_type=jnp.float32)
        attended = lax.dynamic_update_slice_in_dim(attended, o_blk, first_row, 0)
        log_row = (row_peak + jnp.log(denominator))[..., 0]
        log_totals = lax.dynamic_update_slice_in_dim(log_totals, log_row, first_row, 1)
        return (attended, log_totals)

    initial = (
        jnp.zeros((length_now, group_heads, head_dim), jnp.float32),
        jnp.zeros((group_heads, length_now), jnp.float32),
    )
    return lax.fori_loop(0, length_now // block_rows, one_block, initial)


def attention_backward(
    queries, pad_keys, pad_values, segments, pad_segments, log_totals, grad_mixed
):
    length_now, group_heads, head_dim = queries.shape
    block_rows = min(512, length_now)
    score_scale = head_dim ** (-0.5)

    def one_block(block_step, running):
        grad_q, grad_k, grad_v = running
        first_row = block_step * block_rows
        q_blk, k_blk, scores = block_scores(
            queries, pad_keys, segments, pad_segments, first_row, block_rows
        )
        v_blk = lax.dynamic_slice_in_dim(pad_values, first_row, block_rows + WINDOW, 0)
        total_rows = lax.dynamic_slice_in_dim(log_totals, first_row, block_rows, 1)
        block_probs = jnp.exp(scores - total_rows[..., None])
        do_blk = lax.dynamic_slice_in_dim(grad_mixed, first_row, block_rows, 0)
        grad_probs = jnp.einsum("qhd,kd->hqk", do_blk, v_blk, preferred_element_type=jnp.float32)
        centred = jnp.sum(block_probs * grad_probs, axis=-1, keepdims=True)
        grad_scores = (score_scale * block_probs * (grad_probs - centred)).astype(jnp.bfloat16)
        grad_q_blk = jnp.einsum(
            "hqk,kd->qhd", grad_scores, k_blk, preferred_element_type=jnp.float32
        )
        grad_k_blk = jnp.einsum(
            "hqk,qhd->kd", grad_scores, q_blk, preferred_element_type=jnp.float32
        )
        grad_v_blk = jnp.einsum(
            "hqk,qhd->kd",
            block_probs.astype(jnp.bfloat16),
            do_blk,
            preferred_element_type=jnp.float32,
        )
        grad_q = lax.dynamic_update_slice_in_dim(grad_q, grad_q_blk, first_row, 0)
        old_k = lax.dynamic_slice_in_dim(grad_k, first_row, block_rows + WINDOW, 0)
        grad_k = lax.dynamic_update_slice_in_dim(grad_k, old_k + grad_k_blk, first_row, 0)
        old_v = lax.dynamic_slice_in_dim(grad_v, first_row, block_rows + WINDOW, 0)
        grad_v = lax.dynamic_update_slice_in_dim(grad_v, old_v + grad_v_blk, first_row, 0)
        return (grad_q, grad_k, grad_v)

    initial = (
        jnp.zeros((length_now, group_heads, head_dim), jnp.float32),
        jnp.zeros((length_now + WINDOW, head_dim), jnp.float32),
        jnp.zeros((length_now + WINDOW, head_dim), jnp.float32),
    )
    return lax.fori_loop(0, length_now // block_rows, one_block, initial)


def per_device(
    tokens, w_query, w_keyval, w_out, w_gate, w_up, w_down, norm_gains, segment_ids, grad_output
):
    fetched = (
        lax.all_gather(w_query, "dp", axis=0, tiled=True),
        lax.all_gather(w_keyval, "dp", axis=0, tiled=True),
        lax.all_gather(w_out, "dp", axis=1, tiled=True),
        lax.all_gather(w_gate, "dp", axis=0, tiled=True),
        lax.all_gather(w_up, "dp", axis=0, tiled=True),
        lax.all_gather(w_down, "dp", axis=1, tiled=True),
        lax.all_gather(norm_gains, "dp", axis=1, tiled=True),
    )
    full_query, full_keyval, full_out, full_gate, full_up, full_down, full_gains = fetched
    gains_float = full_gains.astype(jnp.float32)
    x_rows = tokens.astype(jnp.float32)
    normed = rms_scaled(x_rows, gains_float[0]).astype(jnp.bfloat16)
    normed_all = lax.all_gather(normed, "tensor", axis=0, tiled=True)
    length_now = normed_all.shape[0]
    head_dim = full_keyval.shape[1] // 2
    group_heads = full_query.shape[1] // head_dim
    q_pre = jnp.dot(normed_all, full_query, preferred_element_type=jnp.float32)
    kv_pre = jnp.dot(normed_all, full_keyval, preferred_element_type=jnp.float32)
    cosine_table, sine_table = rotary_tables(positions_of(segment_ids), head_dim)
    queries = rotary(
        q_pre.reshape(length_now, group_heads, head_dim),
        cosine_table[:, None, :],
        sine_table[:, None, :],
    ).astype(jnp.bfloat16)
    key_rows = rotary(kv_pre[:, :head_dim], cosine_table, sine_table).astype(jnp.bfloat16)
    value_rows = kv_pre[:, head_dim:].astype(jnp.bfloat16)
    pad_keys = jnp.concatenate([jnp.zeros((WINDOW, head_dim), jnp.bfloat16), key_rows])
    pad_values = jnp.concatenate([jnp.zeros((WINDOW, head_dim), jnp.bfloat16), value_rows])
    pad_segments = jnp.concatenate([jnp.full((WINDOW,), -1, jnp.int32), segment_ids])
    attended, log_totals = attention_forward(
        queries, pad_keys, pad_values, segment_ids, pad_segments
    )
    valid_rows = (segment_ids != 0).astype(jnp.float32)[:, None]
    mixed_heads = (attended.reshape(length_now, group_heads * head_dim) * valid_rows).astype(
        jnp.bfloat16
    )
    attn_sum = lax.psum_scatter(
        jnp.dot(mixed_heads, full_out, preferred_element_type=jnp.float32),
        "tensor",
        scatter_dimension=0,
        tiled=True,
    )
    residual = x_rows + attn_sum
    normed_two = rms_scaled(residual, gains_float[1]).astype(jnp.bfloat16)
    normed_two_all = lax.all_gather(normed_two, "tensor", axis=0, tiled=True)
    gate_act = jnp.dot(normed_two_all, full_gate, preferred_element_type=jnp.float32)
    up_act = jnp.dot(normed_two_all, full_up, preferred_element_type=jnp.float32)
    hidden = gated_gelu(gate_act, up_act).astype(jnp.bfloat16)
    ffn_sum = lax.psum_scatter(
        jnp.dot(hidden, full_down, preferred_element_type=jnp.float32).astype(jnp.bfloat16),
        "tensor",
        scatter_dimension=0,
        tiled=True,
    ).astype(jnp.float32)
    output = (residual + ffn_sum).astype(jnp.bfloat16)
    again_shards = lax.optimization_barrier(
        (w_query, w_keyval, w_out, w_gate, w_up, w_down, norm_gains, output)
    )
    refetched = (
        lax.all_gather(again_shards[0], "dp", axis=0, tiled=True),
        lax.all_gather(again_shards[1], "dp", axis=0, tiled=True),
        lax.all_gather(again_shards[2], "dp", axis=1, tiled=True),
        lax.all_gather(again_shards[3], "dp", axis=0, tiled=True),
        lax.all_gather(again_shards[4], "dp", axis=0, tiled=True),
        lax.all_gather(again_shards[5], "dp", axis=1, tiled=True),
        lax.all_gather(again_shards[6], "dp", axis=1, tiled=True),
    )
    back_query, back_keyval, back_out, back_gate, back_up, back_down, back_gains = refetched
    back_gains_float = back_gains.astype(jnp.float32)
    grad_ffn = lax.all_gather(grad_output.astype(jnp.bfloat16), "tensor", axis=0, tiled=True)
    grad_hidden = contract_last(grad_ffn, back_down)
    grad_w_down = contract_first(hidden, grad_ffn)
    _, gated_back = jax.vjp(gated_gelu, gate_act, up_act)
    grad_gate_f, grad_up_f = gated_back(grad_hidden)
    grad_gate = grad_gate_f.astype(jnp.bfloat16)
    grad_up = grad_up_f.astype(jnp.bfloat16)
    grad_w_gate = contract_first(normed_two_all, grad_gate)
    grad_w_up = contract_first(normed_two_all, grad_up)
    grad_normed_two = lax.psum_scatter(
        contract_last(grad_gate, back_gate) + contract_last(grad_up, back_up),
        "tensor",
        scatter_dimension=0,
        tiled=True,
    )
    _, norm_back = jax.vjp(rms_scaled, residual, back_gains_float[1])
    grad_res_part, gain_two = norm_back(grad_normed_two)
    grad_residual = grad_output + grad_res_part
    grad_attn = lax.all_gather(grad_residual.astype(jnp.bfloat16), "tensor", axis=0, tiled=True)
    grad_w_out = contract_first(mixed_heads, grad_attn)
    grad_mixed = (contract_last(grad_attn, back_out) * valid_rows).astype(jnp.bfloat16)
    grad_mixed = grad_mixed.reshape(length_now, group_heads, head_dim)
    grad_queries, grad_pad_keys, grad_pad_values = attention_backward(
        queries, pad_keys, pad_values, segment_ids, pad_segments, log_totals, grad_mixed
    )
    grad_q_pre = rotary(grad_queries, cosine_table[:, None, :], -sine_table[:, None, :])
    grad_q_pre = grad_q_pre.reshape(length_now, group_heads * head_dim).astype(jnp.bfloat16)
    grad_k_pre = rotary(grad_pad_keys[WINDOW:], cosine_table, -sine_table)
    grad_kv = jnp.concatenate([grad_k_pre, grad_pad_values[WINDOW:]], axis=1).astype(jnp.bfloat16)
    grad_w_query = contract_first(normed_all, grad_q_pre)
    grad_w_keyval = contract_first(normed_all, grad_kv)
    grad_normed = lax.psum_scatter(
        (contract_last(grad_q_pre, back_query) + contract_last(grad_kv, back_keyval)).astype(
            jnp.bfloat16
        ),
        "tensor",
        scatter_dimension=0,
        tiled=True,
    ).astype(jnp.float32)
    _, first_back = jax.vjp(rms_scaled, x_rows, back_gains_float[0])
    grad_x_part, gain_one = first_back(grad_normed)
    grad_tokens = grad_residual + grad_x_part
    grad_gains = jnp.stack([gain_one, gain_two])
    shards = (
        lax.psum_scatter(grad_w_query, "dp", scatter_dimension=0, tiled=True),
        lax.psum_scatter(grad_w_keyval, "dp", scatter_dimension=0, tiled=True),
        lax.psum_scatter(grad_w_out, "dp", scatter_dimension=1, tiled=True),
        lax.psum_scatter(grad_w_gate, "dp", scatter_dimension=0, tiled=True),
        lax.psum_scatter(grad_w_up, "dp", scatter_dimension=0, tiled=True),
        lax.psum_scatter(grad_w_down, "dp", scatter_dimension=1, tiled=True),
        lax.psum_scatter(grad_gains, "dp", scatter_dimension=1, tiled=True),
    )
    keyval_shard, gains_shard = lax.psum((shards[1], shards[6]), "tensor")
    return (
        output,
        grad_tokens,
        shards[0],
        keyval_shard,
        shards[2],
        shards[3],
        shards[4],
        shards[5],
        gains_shard,
    )


def solution(mesh):
    return jax.shard_map(
        per_device,
        mesh=mesh,
        in_specs=(
            P(("dp", "tensor"), None),
            P("dp", "tensor"),
            P("dp", None),
            P("tensor", "dp"),
            P("dp", "tensor"),
            P("dp", "tensor"),
            P("tensor", "dp"),
            P(None, "dp"),
            P("dp"),
            P(("dp", "tensor"), None),
        ),
        out_specs=(
            P(("dp", "tensor"), None),
            P(("dp", "tensor"), None),
            P("dp", "tensor"),
            P("dp", None),
            P("tensor", "dp"),
            P("dp", "tensor"),
            P("dp", "tensor"),
            P("tensor", "dp"),
            P(None, "dp"),
        ),
        check_vma=False,
    )
```

profile of v0, /device:TPU:0, one launch (start us, length us, event | category | flops | bytes accessed | tf_op | source)
XLA Modules:
  0.0 2004.0 jit_solution(9522569689751602551)
XLA Ops:
  9.1 22.5 %all-gather = bf16[8,192,2]{1,2,0:T(2,128)(2,1)S(1)} all-gather(bf16[1,192,2]{1,2,0:T(2,128)(2,1)} %bitcast.178), channel_id=1, replica_groups=mesh['dp'=8,'tensor'=4] {'dp'}, dimensions={0}, use_global_device_ids=true | all-gather | bytes 6912 | tf_op jit(solution)/shard_map/all_gather | solution.py:166
  37.0 32.3 %all_gather.56 = bf16[1536,256]{1,0:T(8,128)(2,1)S(1)} all-gather(bf16[192,256]{1,0:T(8,128)(2,1)S(1)} %copy-done.16), channel_id=1, replica_groups=mesh['dp'=8,'tensor'=4] {'dp'}, dimensions={0}, use_global_device_ids=true | all-gather | bytes 884736 | tf_op jit(solution)/shard_map/all_gather | solution.py:161
  86.8 35.0 %all-gather.19.cloned.1.call-done = bf16[1536,384]{1,0:T(8,128)(2,1)} async-done(((bf16[192,384]{1,0:T(8,128)(2,1)}), bf16[1536,384]{1,0:T(8,128)(2,1)}) %all-gather.19.cloned.1.call-update) | async-done | bytes 1179664 | tf_op jit(solution)/shard_map/all_gather | solution.py:160
  132.8 37.6 %while.36 = (s32[]{:T(128)}, f32[2048,3,128]{0,2,1:T(8,128)}, f32[3,2048]{1,0:T(4,128)S(1)}, bf16[3072,128]{0,1:T(8,128)(2,1)S(1)}, s32[2048]{0:T(1024)S(1)}, /*...) while((s32[]{:T(128)}, f32[2048,3,128]{0,2,1:T(8,128)}, ...), condition=%wide.region_6.7_spmd, body=%wide.region_3.0_spmd.sunk | while | flops 1240990208 | bytes 33523964 | solution.py:106
  185.4 97.3 %reduce-scatter.14.cloned.1.call-done = f32[512,1536]{1,0:T(8,128)} async-done(((f32[2048,1536]{1,0:T(8,128)}), f32[512,1536]{1,0:T(8,128)}) %reduce-scatter.14.cloned.1.call-update) | async-done | bytes 3145744 | tf_op jit(solution)/shard_map/reduce_scatter | solution.py:196
  288.6 61.4 %all-gather.25.cloned.1.call-done = bf16[1536,1152]{1,0:T(8,128)(2,1)} async-done(((bf16[192,1152]{1,0:T(8,128)(2,1)}), bf16[1536,1152]{1,0:T(8,128)(2,1)}) %all-gather.25.cloned.1.call-update) | async-done | bytes 3538960 | tf_op jit(solution)/shard_map/all_gather | solution.py:163
  350.0 46.9 %all-gather.23.cloned.1.call-done = bf16[2048,1536]{1,0:T(8,128)(2,1)} async-done(((bf16[512,1536]{1,0:T(8,128)(2,1)}), bf16[2048,1536]{1,0:T(8,128)(2,1)}) %all-gather.23.cloned.1.call-update) | async-done | bytes 6291472 | tf_op jit(solution)/shard_map/all_gather | solution.py:204
  410.4 53.9 %all-gather.27.cloned.1.call-done = bf16[1536,1152]{1,0:T(8,128)(2,1)} async-done(((bf16[192,1152]{1,0:T(8,128)(2,1)}), bf16[1536,1152]{1,0:T(8,128)(2,1)}) %all-gather.27.cloned.1.call-update) | async-done | bytes 3538960 | tf_op jit(solution)/shard_map/all_gather | solution.py:164
  464.3 16.5 multiply_convert_fusion
  480.8 49.4 %all-gather.29.cloned.1.call-done = bf16[1152,1536]{0,1:T(8,128)(2,1)} async-done(((bf16[1152,192]{0,1:T(8,128)(2,1)}), bf16[1152,1536]{0,1:T(8,128)(2,1)}) %all-gather.29.cloned.1.call-update) | async-done | bytes 3538960 | tf_op jit(solution)/shard_map/all_gather | solution.py:165
  546.8 53.7 %reduce-scatter.16.cloned.1.call-done = bf16[512,1536]{1,0:T(8,128)(2,1)} async-done(((bf16[2048,1536]{1,0:T(8,128)(2,1)}), bf16[512,1536]{1,0:T(8,128)(2,1)}) %reduce-scatter.16.cloned.1.call-update) | async-done | bytes 1572880 | tf_op jit(solution)/shard_map/reduce_scatter | solution.py:208
  604.9 44.1 %all-gather.33.cloned.1.call-done = bf16[2048,1536]{1,0:T(8,128)(2,1)} async-done(((bf16[512,1536]{1,0:T(8,128)(2,1)}), bf16[2048,1536]{1,0:T(8,128)(2,1)}) %all-gather.33.cloned.1.call-update) | async-done | bytes 6291472 | tf_op jit(solution)/shard_map/all_gather | solution.py:229
  649.0 67.6 %all-gather.31.cloned.1.call-done = bf16[1152,1536]{0,1:T(8,128)(2,1)} async-done(((bf16[1152,192]{0,1:T(8,128)(2,1)}), bf16[1152,1536]{0,1:T(8,128)(2,1)}) %all-gather.31.cloned.1.call-update) | async-done | bytes 3538960 | tf_op jit(solution)/shard_map/all_gather | solution.py:224
  716.6 23.0 %fusion.60 = (bf16[2048,1152]{1,0:T(8,128)(2,1)}, bf16[2048,1152]{1,0:T(8,128)(2,1)}) fusion(f32[2048,1152]{1,0:T(8,128)} %fusion.96, f32[2048,1152]{1,0:T(8,128)} %get-tuple-element.639, bf16[2048,1536]{1,0:T(8,128)(2,1)} %all-gather.33.cloned.1.call-done, bf16[1152,1536]{0,1:T(8,128)(2,1)} %all-gather.31.cloned.1.call-done), kind=kOutput, calls=%fused_computation.79 | convolution fusion | flops 7304380416 | bytes 38141952 | tf_op jit(solution)/shard_map/dot_general | solution.py:50
  739.6 43.0 %all-gather.35.cloned.1.call-done = bf16[1536,1152]{1,0:T(8,128)(2,1)} async-done(((bf16[192,1152]{1,0:T(8,128)(2,1)}), bf16[1536,1152]{1,0:T(8,128)(2,1)}) %all-gather.35.cloned.1.call-update) | async-done | bytes 3538960 | tf_op jit(solution)/shard_map/all_gather | solution.py:222
  782.6 14.2 fusion.97
  796.8 52.0 %all-gather.37.cloned.1.call-done = bf16[1536,1152]{1,0:T(8,128)(2,1)} async-done(((bf16[192,1152]{1,0:T(8,128)(2,1)}), bf16[1536,1152]{1,0:T(8,128)(2,1)}) %all-gather.37.cloned.1.call-update) | async-done | bytes 3538960 | tf_op jit(solution)/shard_map/all_gather | solution.py:223
  848.7 16.2 convolution_add_fusion
  865.6 18.1 all-gather.1
  884.4 78.3 %reduce-scatter.18.cloned.1.call-done = f32[512,1536]{1,0:T(8,128)} async-done(((f32[2048,1536]{1,0:T(8,128)}), f32[512,1536]{1,0:T(8,128)}) %reduce-scatter.18.cloned.1.call-update) | async-done | bytes 3145744 | tf_op jit(solution)/shard_map/reduce_scatter | solution.py:238
  969.5 35.2 %all_gather.71 = bf16[1536,256]{1,0:T(8,128)(2,1)} all-gather(bf16[192,256]{1,0:T(8,128)(2,1)S(1)} %copy-done.17), channel_id=1, replica_groups=mesh['dp'=8,'tensor'=4] {'dp'}, dimensions={0}, use_global_device_ids=true | all-gather | bytes 884736 | tf_op jit(solution)/shard_map/all_gather | solution.py:220
  1011.0 46.4 %all-gather.39.cloned.1.call-done = bf16[2048,1536]{1,0:T(8,128)(2,1)} async-done(((bf16[512,1536]{1,0:T(8,128)(2,1)}), bf16[2048,1536]{1,0:T(8,128)(2,1)}) %all-gather.39.cloned.1.call-update) | async-done | bytes 6291472 | tf_op jit(solution)/shard_map/all_gather | solution.py:247
  1068.9 140.6 %while.37 = (s32[]{:T(128)}, f32[2048,3,128]{0,2,1:T(8,128)}, f32[3072,128]{0,1:T(8,128)}, f32[3072,128]{1,0:T(8,128)}, bf16[3072,128]{1,0:T(8,128)(2,1)S(1)}, /...) while((s32[]{:T(128)}, f32[2048,3,128]{0,2,1:T(8,128)}, ...), condition=%wide.region_14.15_spmd, body=%wide.region_12.14_spmd.sunk | while | flops 3048604160 | bytes 142025040 | solution.py:153
  1234.4 52.1 %reduce-scatter.20.cloned.1.call-done = bf16[512,1536]{1,0:T(8,128)(2,1)} async-done(((bf16[2048,1536]{1,0:T(8,128)(2,1)}), bf16[512,1536]{1,0:T(8,128)(2,1)}) %reduce-scatter.20.cloned.1.call-update) | async-done | bytes 1572880 | tf_op jit(solution)/shard_map/reduce_scatter | solution.py:260
  1332.4 22.4 %reduce-scatter.24.cloned.1.call-done = f32[192,256]{1,0:T(8,128)} async-done(((f32[1536,256]{1,0:T(8,128)}), f32[192,256]{1,0:T(8,128)}) %reduce-scatter.24.cloned.1.call-update) | async-done | bytes 196624 | tf_op jit(solution)/shard_map/reduce_scatter | solution.py:274
  1376.9 42.6 %reduce-scatter.34.cloned.1.call-done = f32[192,2]{1,0:T(8,128)} async-done(((f32[1536,2]{1,0:T(8,128)}), f32[192,2]{1,0:T(8,128)}) %reduce-scatter.34.cloned.1.call-update) | async-done | bytes 1552
  1426.7 125.1 %reduce-scatter.32.cloned.1.call-done = f32[1152,192]{0,1:T(8,128)} async-done(((f32[1152,1536]{0,1:T(8,128)}), f32[1152,192]{0,1:T(8,128)}) %reduce-scatter.32.cloned.1.call-update) | async-done | bytes 884752 | tf_op jit(solution)/shard_map/reduce_scatter | solution.py:278
  1551.8 132.8 %reduce-scatter.30.cloned.1.call-done = f32[192,1152]{1,0:T(8,128)} async-done(((f32[1536,1152]{1,0:T(8,128)}), f32[192,1152]{1,0:T(8,128)}) %reduce-scatter.30.cloned.1.call-update) | async-done | bytes 884752 | tf_op jit(solution)/shard_map/reduce_scatter | solution.py:277
  1684.6 132.3 %reduce-scatter.28.cloned.1.call-done = f32[192,1152]{1,0:T(8,128)} async-done(((f32[1536,1152]{1,0:T(8,128)}), f32[192,1152]{1,0:T(8,128)}) %reduce-scatter.28.cloned.1.call-update) | async-done | bytes 884752 | tf_op jit(solution)/shard_map/reduce_scatter | solution.py:276
  1817.0 33.1 %all-reduce.5.cloned.1.call-done = f32[192,256]{1,0:T(8,128)} async-done(((f32[192,256]{1,0:T(8,128)}), f32[192,256]{1,0:T(8,128)}) %all-reduce.5.cloned.1.call-update) | async-done | bytes 196624 | tf_op jit(solution)/shard_map/psum | solution.py:281
  1850.0 73.1 %reduce-scatter.26.cloned.1.call-done = f32[384,192]{0,1:T(8,128)} async-done(((f32[384,1536]{0,1:T(8,128)}), f32[384,192]{0,1:T(8,128)}) %reduce-scatter.26.cloned.1.call-update) | async-done | bytes 294928 | tf_op jit(solution)/shard_map/reduce_scatter | solution.py:275
  1923.1 72.2 %reduce-scatter.22.cloned.1.call-done = f32[192,384]{1,0:T(8,128)} async-done(((f32[1536,384]{1,0:T(8,128)}), f32[192,384]{1,0:T(8,128)}) %reduce-scatter.22.cloned.1.call-update) | async-done | bytes 294928 | tf_op jit(solution)/shard_map/reduce_scatter | solution.py:273
  (299 shorter events, 395.4 us)
Async XLA Ops:
  7.2 71.4 %all-gather.17.cloned.1.call-start = ((), (), s32[]{:S(2)}) async-start(), calls=%async_computation.11 | async-start | bytes 7864320 | tf_op jit(solution)/shard_map/all_gather | solution.py:172
  9.0 74.2 %copy-start.25 = (f32[512]{0:T(512)}, f32[512]{0:T(512)S(1)}, u32[]{:S(2)}) copy-start(f32[512]{0:T(512)S(1)} %fusion.67) | copy-start | bytes 6148
  9.1 74.1 %copy-start.23 = (f32[512]{0:T(512)}, f32[512]{0:T(512)S(1)}, u32[]{:S(2)}) copy-start(f32[512]{0:T(512)S(1)} %fusion.87) | copy-start | bytes 6148
  34.7 87.1 %all-gather.19.cloned.1.call-start = ((), (), s32[]{:S(2)}) async-start(), calls=%async_computation.12 | async-start | bytes 1327104 | tf_op jit(solution)/shard_map/all_gather | solution.py:160
  35.5 139.4 %all-gather.21.cloned.1.call-start = ((), (), s32[]{:S(2)}) async-start(), calls=%async_computation.13 | async-start | bytes 1327104 | tf_op jit(solution)/shard_map/all_gather | solution.py:162
  36.2 246.5 %reduce-scatter.14.cloned.1.call-start = ((), (), s32[]{:S(2)}) async-start(), calls=%async_computation.14 | async-start | bytes 15728640 | tf_op jit(solution)/shard_map/reduce_scatter | solution.py:196
  184.8 165.2 %all-gather.25.cloned.1.call-start = ((), (), s32[]{:S(2)}) async-start(), calls=%async_computation.16 | async-start | bytes 3981312 | tf_op jit(solution)/shard_map/all_gather | solution.py:163
  185.4 211.5 %all-gather.23.cloned.1.call-start = ((), (), s32[]{:S(2)}) async-start(), calls=%async_computation.15 | async-start | bytes 7864320 | tf_op jit(solution)/shard_map/all_gather | solution.py:204
  287.1 177.2 %all-gather.27.cloned.1.call-start = ((), (), s32[]{:S(2)}) async-start(), calls=%async_computation.17 | async-start | bytes 3981312 | tf_op jit(solution)/shard_map/all_gather | solution.py:164
  287.8 242.4 %all-gather.29.cloned.1.call-start = ((), (), s32[]{:S(2)}) async-start(), calls=%async_computation.18 | async-start | bytes 3981312 | tf_op jit(solution)/shard_map/all_gather | solution.py:165
  288.6 311.9 %reduce-scatter.16.cloned.1.call-start = ((), (), s32[]{:S(2)}) async-start(), calls=%async_computation.19 | async-start | bytes 7864320 | tf_op jit(solution)/shard_map/reduce_scatter | solution.py:208
  543.5 105.5 %all-gather.33.cloned.1.call-start = ((), (), s32[]{:S(2)}) async-start(), calls=%async_computation.21 | async-start | bytes 7864320 | tf_op jit(solution)/shard_map/all_gather | solution.py:229
  546.8 169.8 %all-gather.31.cloned.1.call-start = ((), (), s32[]{:S(2)}) async-start(), calls=%async_computation.20 | async-start | bytes 3981312 | tf_op jit(solution)/shard_map/all_gather | solution.py:224
  603.5 179.1 %all-gather.35.cloned.1.call-start = ((), (), s32[]{:S(2)}) async-start(), calls=%async_computation.22 | async-start | bytes 3981312 | tf_op jit(solution)/shard_map/all_gather | solution.py:222
  604.1 244.6 %all-gather.37.cloned.1.call-start = ((), (), s32[]{:S(2)}) async-start(), calls=%async_computation.23 | async-start | bytes 3981312 | tf_op jit(solution)/shard_map/all_gather | solution.py:223
  604.9 357.7 %reduce-scatter.18.cloned.1.call-start = ((), (), s32[]{:S(2)}) async-start(), calls=%async_computation.24 | async-start | bytes 15728640 | tf_op jit(solution)/shard_map/reduce_scatter | solution.py:238
  864.9 146.1 %all-gather.41.cloned.1.call-start = ((), (), s32[]{:S(2)}) async-start(), calls=%async_computation.26 | async-start | bytes 1327104 | tf_op jit(solution)/shard_map/all_gather | solution.py:221
  865.5 191.8 %all-gather.39.cloned.1.call-start = ((), (), s32[]{:S(2)}) async-start(), calls=%async_computation.25 | async-start | bytes 7864320 | tf_op jit(solution)/shard_map/all_gather | solution.py:247
  969.4 248.6 %all-gather.43.cloned.1.call-start = ((), (), s32[]{:S(2)}) async-start(), calls=%async_computation.27 | async-start | bytes 1327104 | tf_op jit(solution)/shard_map/all_gather | solution.py:219
  1004.7 281.8 %reduce-scatter.20.cloned.1.call-start = ((), (), s32[]{:S(2)}) async-start(), calls=%async_computation.28 | async-start | bytes 7864320 | tf_op jit(solution)/shard_map/reduce_scatter | solution.py:260
  1068.9 142.0 %copy-start.21 = (f32[2048]{0:T(1024)S(1)}, f32[2048]{0:T(1024)}, u32[]{:S(2)}) copy-start(f32[2048]{0:T(1024)} %copy-done.20) | copy-start | bytes 24580
  1068.9 142.0 %copy-start.29 = (f32[64]{0:T(128)S(1)}, f32[64]{0:T(128)}, u32[]{:S(2)}) copy-start(f32[64]{0:T(128)} %copy-done.28) | copy-start | bytes 772
  1228.0 58.5 %copy-start.2 = (bf16[512,1536]{1,0:T(8,128)(2,1)S(1)}, bf16[512,1536]{1,0:T(8,128)(2,1)}, u32[]{:S(2)}) copy-start(bf16[512,1536]{1,0:T(8,128)(2,1)} %param.14) | copy-start | bytes 4718596
  1228.0 58.5 %copy-start.19 = (f32[1536]{0:T(1024)S(1)}, f32[1536]{0:T(1024)}, u32[]{:S(2)}) copy-start(f32[1536]{0:T(1024)} %get-tuple-element.573) | copy-start | bytes 18436
  1228.0 126.7 %reduce-scatter.24.cloned.1.call-start = ((), (), s32[]{:S(2)}) async-start(), calls=%async_computation.30 | async-start | bytes 1769472 | tf_op jit(solution)/shard_map/reduce_scatter | solution.py:274
  1234.3 185.2 %reduce-scatter.34.cloned.1.call-start = ((), (), s32[]{:S(2)}) async-start(), calls=%async_computation.36 | async-start | bytes 884736
  1290.4 261.4 %reduce-scatter.32.cloned.1.call-start = ((), (), s32[]{:S(2)}) async-start(), calls=%async_computation.35 | async-start | bytes 7962624 | tf_op jit(solution)/shard_map/reduce_scatter | solution.py:278
  1304.3 380.3 %reduce-scatter.30.cloned.1.call-start = ((), (), s32[]{:S(2)}) async-start(), calls=%async_computation.34 | async-start | bytes 7962624 | tf_op jit(solution)/shard_map/reduce_scatter | solution.py:277
  1318.2 498.8 %reduce-scatter.28.cloned.1.call-start = ((), (), s32[]{:S(2)}) async-start(), calls=%async_computation.33 | async-start | bytes 7962624 | tf_op jit(solution)/shard_map/reduce_scatter | solution.py:276
  1332.3 517.7 %all-reduce.5.cloned.1.call-start = ((), (), s32[]{:S(2)}) async-start(), calls=%async_computation.31 | async-start | bytes 393216 | tf_op jit(solution)/shard_map/psum | solution.py:281
  1354.7 568.4 %reduce-scatter.26.cloned.1.call-start = ((), (), s32[]{:S(2)}) async-start(), calls=%async_computation.32 | async-start | bytes 2654208 | tf_op jit(solution)/shard_map/reduce_scatter | solution.py:275
  1362.6 632.8 %reduce-scatter.22.cloned.1.call-start = ((), (), s32[]{:S(2)}) async-start(), calls=%async_computation.29 | async-start | bytes 2654208 | tf_op jit(solution)/shard_map/reduce_scatter | solution.py:273
  (30 other events, 424.0 us)
Sparse Core Ops, SparseCore 0:
  34.8 43.6 all-gather.16
  80.7 41.0 all-gather.18
  124.0 39.8 all-gather.20
  184.9 97.7 reduce-scatter.13
  284.8 65.1 all-gather.24
  352.0 44.8 all-gather.22
  399.1 65.1 all-gather.26
  466.5 63.6 all-gather.28
  543.6 56.8 reduce-scatter.15
  602.6 46.3 all-gather.32
  651.4 65.1 all-gather.30
  718.9 63.6 all-gather.34
  785.0 63.6 all-gather.36
  865.0 97.5 reduce-scatter.17
  964.9 46.0 all-gather.40
  1012.5 44.8 all-gather.38
  1059.6 41.0 all-gather.42
  1228.1 58.3 reduce-scatter.19
  1289.9 64.7 reduce-scatter.23
  1358.2 61.2 reduce-scatter.33
  1423.8 127.9 reduce-scatter.31
  1556.5 128.0 reduce-scatter.29
  1688.9 128.0 reduce-scatter.27
  1819.3 30.7 all-reduce.4
  1854.1 68.9 reduce-scatter.25
  1927.0 68.2 reduce-scatter.21
where the time goes:
time: 2010 us; the launch traced here: 2000 us
  waiting for transfers between devices  1440 us (72%)
  matrix products  300 us (15%)
  blocking collectives  114 us (6%)
  other arithmetic  107 us (5%)
  local copies, waits for them, and re-layouts  29.6 us (1%)
    reduce_scatter x1, waiting for transfers between devices, per_device(): lax.psum_scatter(grad_w_up, 'dp', scatter_dimension=0, tiled=True)  133 us
    reduce_scatter x1, waiting for transfers between devices, per_device(): lax.psum_scatter(grad_w_gate, 'dp', scatter_dimension=0, tiled=True)  132 us
    reduce_scatter x1, waiting for transfers between devices, per_device(): lax.psum_scatter(grad_w_down, 'dp', scatter_dimension=1, tiled=True)  125 us
    reduce_scatter x1, waiting for transfers between devices, per_device(): lax.psum_scatter(jnp.dot(mixed_heads, full_out, preferred_element_type=jn...  97.3 us
    reduce_scatter x1, waiting for transfers between devices, per_device(): lax.psum_scatter(contract_last(grad_gate, back_gate) + contract_last(grad...  78.3 us
    reduce_scatter x1, waiting for transfers between devices, per_device(): lax.psum_scatter(grad_w_out, 'dp', scatter_dimension=1, tiled=True)  73.1 us
    reduce_scatter x1, waiting for transfers between devices, per_device(): lax.psum_scatter(grad_w_query, 'dp', scatter_dimension=0, tiled=True)  72.2 us
    dot_general x6, matrix products, contract_last(): lax.dot_general(left, right, (((1,), (1,)), ((), ())), preferred_element_...  70.1 us
  transfers between devices with their start and end apart: 26, of which 24 were waited for; matrix products, arithmetic and copies ran while one was open for 19% of the time, Pallas kernels for 0%

commit v1 on v0

v1 whole, which is shorter than its diff:
```python
import functools

import jax
import jax.numpy as jnp
from jax import lax
from jax.experimental import pallas as pl
from jax.experimental.pallas import tpu as pltpu
from jax.sharding import PartitionSpec as P

WINDOW = 1024
EPS = 1e-6
MASKED = -1e30
HEAD = 128
BLK = 256
LOG2E = 1.4426950408889634
F32 = jnp.float32
BF16 = jnp.bfloat16
MIB = 1 << 20

NT = (((1,), (1,)), ((), ()))
TN = (((0,), (0,)), ((), ()))


def dot(left, right):
    return jnp.dot(left, right, preferred_element_type=F32)


def dot_nt(left, right):
    return lax.dot_general(left, right, NT, preferred_element_type=F32)


def dot_tn(left, right):
    return lax.dot_general(left, right, TN, preferred_element_type=F32)


def qkv_kernel(x0, x1, x2, x3, gain, w, cos, sin, normed, q, k, v, held):
    i = pl.program_id(0)
    per = pl.num_programs(0) // 4
    for j, ref in enumerate((x0, x1, x2, x3)):

        @pl.when(i // per == j)
        def _(ref=ref):
            held[...] = ref[...]

    rows = held[...].astype(F32)
    scale = lax.rsqrt(jnp.mean(rows * rows, axis=-1, keepdims=True) + EPS)
    n = (rows * scale * gain[...]).astype(BF16)
    normed[...] = n
    y = dot(n, w[...])
    c, s = cos[...], sin[...]
    heads = q.shape[1] // HEAD

    def turned(a):
        return (a * c + pltpu.roll(a, HEAD // 2, 1) * s).astype(BF16)

    for h in range(heads):
        q[:, h * HEAD : (h + 1) * HEAD] = turned(y[:, h * HEAD : (h + 1) * HEAD])
    at = heads * HEAD
    k[...] = turned(y[:, at : at + HEAD])
    v[...] = y[:, at + HEAD : at + 2 * HEAD].astype(BF16)


def project(parts, gain, weights, cos, sin, q_cols):
    quarter, width = parts[0].shape
    rows = 4 * quarter
    per = quarter // BLK
    cols = q_cols + 2 * HEAD

    def part_spec(j):
        return pl.BlockSpec((BLK, width), lambda i: (jnp.clip(i - j * per, 0, per - 1), 0))

    def row_spec(n):
        return pl.BlockSpec((BLK, n), lambda i: (i, 0))

    return pl.pallas_call(
        qkv_kernel,
        grid=(rows // BLK,),
        in_specs=[part_spec(j) for j in range(4)]
        + [
            pl.BlockSpec((1, width), lambda i: (0, 0)),
            pl.BlockSpec((width, cols), lambda i: (0, 0)),
            row_spec(HEAD),
            row_spec(HEAD),
        ],
        out_specs=[row_spec(width), row_spec(q_cols), row_spec(HEAD), row_spec(HEAD)],
        out_shape=[
            jax.ShapeDtypeStruct((rows, width), BF16),
            jax.ShapeDtypeStruct((rows, q_cols), BF16),
            jax.ShapeDtypeStruct((rows, HEAD), BF16),
            jax.ShapeDtypeStruct((rows, HEAD), BF16),
        ],
        scratch_shapes=[pltpu.VMEM((BLK, width), BF16)],
        compiler_params=pltpu.CompilerParams(vmem_limit_bytes=32 * MIB),
        cost_estimate=pl.CostEstimate(
            flops=2 * rows * width * cols, bytes_accessed=4 * rows * width, transcendentals=0
        ),
        name="project",
    )(*parts, gain, weights, cos, sin)


def stacked(block, heads):
    return jnp.concatenate([block[:, h * HEAD : (h + 1) * HEAD] for h in range(heads)], axis=0)


def key_row(t, kb):
    per = 512 // BLK
    return pl.multiple_of(((t ^ (kb // per)) * per + kb % per) * BLK, BLK)


def query_block(t, i):
    per = 512 // BLK
    return (t ^ (i // per)) * per + i % per


def tiled3(row, heads):
    return jnp.concatenate([row] * heads, axis=1)


def attn_fwd_kernel(first, t_ref, q, k, v, pos, valid, mixed, lse):
    heads = q.shape[1] // HEAD
    wide = heads * BLK
    t = t_ref[0]
    qb = query_block(t, pl.program_id(0) + first)
    q3 = stacked(q[...], heads)
    at = qb * BLK + lax.broadcasted_iota(jnp.int32, (1, BLK), 1)
    low = at - jnp.minimum(pos[0], WINDOW - 1)
    at3, low3 = tiled3(at, heads), tiled3(low, heads)
    factor = HEAD**-0.5 * LOG2E

    def step(kb, carry):
        peak, total, acc = carry
        row = key_row(t, kb)
        s = dot_nt(k[pl.ds(row, BLK), :], q3) * factor
        u = kb * BLK + lax.broadcasted_iota(jnp.int32, (BLK, wide), 0)
        s = jnp.where((u <= at3) & (u >= low3), s, MASKED)
        new_peak = jnp.maximum(peak, jnp.max(s, axis=0, keepdims=True))
        p = jnp.exp2(s - new_peak)
        shrink = jnp.exp2(peak - new_peak)
        total = total * shrink + jnp.sum(p, axis=0, keepdims=True)
        acc = acc * shrink + dot_tn(v[pl.ds(row, BLK), :], p.astype(BF16))
        return new_peak, total, acc

    peak, total, acc = lax.fori_loop(
        jnp.maximum(qb - WINDOW // BLK, 0),
        qb + 1,
        step,
        (
            jnp.full((1, wide), MASKED, F32),
            jnp.zeros((1, wide), F32),
            jnp.zeros((HEAD, wide), F32),
        ),
    )
    lse[0] = peak + jnp.log2(total)
    acc = acc * (tiled3(valid[0], heads) / total)
    for h in range(heads):
        mixed[:, h * HEAD : (h + 1) * HEAD] = acc[:, h * BLK : (h + 1) * BLK].T.astype(BF16)


def attention_forward(t, q, k, v, pos, valid, first_row, rows):
    cols = q.shape[1]
    heads = cols // HEAD
    first = first_row // BLK
    blocks = rows // BLK
    full = pl.BlockSpec((k.shape[0], HEAD), lambda i, t: (0, 0))
    lane = pl.BlockSpec((1, 1, BLK), lambda i, t: (i + first, 0, 0))
    return pl.pallas_call(
        functools.partial(attn_fwd_kernel, first),
        grid_spec=pltpu.PrefetchScalarGridSpec(
            num_scalar_prefetch=1,
            grid=(blocks,),
            in_specs=[
                pl.BlockSpec((BLK, cols), lambda i, t: (i + first, 0)),
                full,
                full,
                lane,
                lane,
            ],
            out_specs=[
                pl.BlockSpec((BLK, cols), lambda i, t: (i, 0)),
                pl.BlockSpec((1, 1, heads * BLK), lambda i, t: (i, 0, 0)),
            ],
        ),
        out_shape=[
            jax.ShapeDtypeStruct((rows, cols), BF16),
            jax.ShapeDtypeStruct((blocks, 1, heads * BLK), F32),
        ],
        compiler_params=pltpu.CompilerParams(vmem_limit_bytes=32 * MIB),
        cost_estimate=pl.CostEstimate(
            flops=8 * rows * WINDOW * cols, bytes_accessed=8 * rows * cols, transcendentals=rows * WINDOW * heads
        ),
        name="attention_forward",
    )(t, q, k, v, pos, valid)


def attn_bwd_kernel(t_ref, q, do, mixed, lse, k, v, pos, cos, sin, cos_all, sin_all, dq, dkv, dk_acc, dv_acc):
    heads = q.shape[1] // HEAD
    wide = heads * BLK
    t = t_ref[0]
    i = pl.program_id(0)
    qb = query_block(t, i)

    @pl.when(i == 0)
    def _():
        dk_acc[...] = jnp.zeros_like(dk_acc)
        dv_acc[...] = jnp.zeros_like(dv_acc)

    q3 = stacked(q[...], heads)
    do3 = stacked(do[...], heads)
    centre3 = do3.astype(F32) * stacked(mixed[...], heads).astype(F32)
    centre = jnp.sum(centre3.T, axis=0, keepdims=True)
    at = qb * BLK + lax.broadcasted_iota(jnp.int32, (1, BLK), 1)
    low = at - jnp.minimum(pos[0], WINDOW - 1)
    at3, low3 = tiled3(at, heads), tiled3(low, heads)
    total = lse[0]
    factor = HEAD**-0.5 * LOG2E

    def step(kb, acc):
        row = key_row(t, kb)
        kblk = k[pl.ds(row, BLK), :]
        vblk = v[pl.ds(row, BLK), :]
        s = dot_nt(kblk, q3) * factor - total
        u = kb * BLK + lax.broadcasted_iota(jnp.int32, (BLK, wide), 0)
        p = jnp.exp2(jnp.where((u <= at3) & (u >= low3), s, MASKED))
        gp = dot_nt(vblk, do3)
        ds = (p * (gp - centre)).astype(BF16)
        dv_acc[pl.ds(row, BLK), :] += dot(p.astype(BF16), do3)
        dk_acc[pl.ds(row, BLK), :] += dot(ds, q3)
        return acc + dot_tn(kblk, ds)

    acc = lax.fori_loop(
        jnp.maximum(qb - WINDOW // BLK, 0), qb + 1, step, jnp.zeros((HEAD, wide), F32)
    )
    scale = HEAD**-0.5
    c, s = cos[...] * scale, sin[...] * scale
    for h in range(heads):
        a = acc[:, h * BLK : (h + 1) * BLK].T
        dq[:, h * HEAD : (h + 1) * HEAD] = (a * c - pltpu.roll(a, HEAD // 2, 1) * s).astype(BF16)

    @pl.when(i == pl.num_programs(0) - 1)
    def _():
        a = dk_acc[...] * scale
        dkv[:, :HEAD] = (a * cos_all[...] - pltpu.roll(a, HEAD // 2, 1) * sin_all[...]).astype(BF16)
        dkv[:, HEAD:] = dv_acc[...].astype(BF16)


def attention_backward(t, q, do, mixed, lse, k, v, pos, cos, sin):
    rows, cols = q.shape
    heads = cols // HEAD
    full = pl.BlockSpec((rows, HEAD), lambda i, t: (0, 0))
    row_q = pl.BlockSpec((BLK, cols), lambda i, t: (i, 0))
    row_h = pl.BlockSpec((BLK, HEAD), lambda i, t: (i, 0))
    return pl.pallas_call(
        attn_bwd_kernel,
        grid_spec=pltpu.PrefetchScalarGridSpec(
            num_scalar_prefetch=1,
            grid=(rows // BLK,),
            in_specs=[
                row_q,
                row_q,
                row_q,
                pl.BlockSpec((1, 1, heads * BLK), lambda i, t: (i, 0, 0)),
                full,
                full,
                pl.BlockSpec((1, 1, BLK), lambda i, t: (i, 0, 0)),
                row_h,
                row_h,
                full,
                full,
            ],
            out_specs=[row_q, pl.BlockSpec((rows, 2 * HEAD), lambda i, t: (0, 0))],
            scratch_shapes=[pltpu.VMEM((rows, HEAD), F32), pltpu.VMEM((rows, HEAD), F32)],
        ),
        out_shape=[
            jax.ShapeDtypeStruct((rows, cols), BF16),
            jax.ShapeDtypeStruct((rows, 2 * HEAD), BF16),
        ],
        compiler_params=pltpu.CompilerParams(vmem_limit_bytes=40 * MIB),
        cost_estimate=pl.CostEstimate(
            flops=20 * rows * WINDOW * cols, bytes_accessed=12 * rows * cols, transcendentals=rows * WINDOW * heads
        ),
        name="attention_backward",
    )(t, q, do, mixed, lse, k, v, pos, cos, sin, cos, sin)


def ffn_kernel(n, w, grad_hidden, hidden, grads):
    half = hidden.shape[1]
    y = dot(n[...], w[...])
    gate, up = y[:, :half], y[:, half:]
    gh = grad_hidden[...]
    root = (2.0 / jnp.pi) ** 0.5
    square = gate * gate
    th = jnp.tanh(root * gate * (1.0 + 0.044715 * square))
    one = 0.5 * (1.0 + th)
    act = gate * one
    slope = one + 0.5 * gate * (1.0 - th * th) * (root * (1.0 + 3.0 * 0.044715 * square))
    hidden[...] = (act * up).astype(BF16)
    grads[:, :half] = (gh * up * slope).astype(BF16)
    grads[:, half:] = (gh * act).astype(BF16)


def ffn_middle(n, w, grad_hidden):
    rows, width = n.shape
    half = grad_hidden.shape[1]

    def row_spec(c):
        return pl.BlockSpec((BLK, c), lambda i: (i, 0))

    return pl.pallas_call(
        ffn_kernel,
        grid=(rows // BLK,),
        in_specs=[row_spec(width), pl.BlockSpec((width, 2 * half), lambda i: (0, 0)), row_spec(half)],
        out_specs=[row_spec(half), row_spec(2 * half)],
        out_shape=[
            jax.ShapeDtypeStruct((rows, half), BF16),
            jax.ShapeDtypeStruct((rows, 2 * half), BF16),
        ],
        compiler_params=pltpu.CompilerParams(vmem_limit_bytes=50 * MIB),
        cost_estimate=pl.CostEstimate(
            flops=4 * rows * width * half, bytes_accessed=14 * rows * width, transcendentals=rows * half
        ),
        name="ffn_middle",
    )(n, w, grad_hidden)


def positions_of(segments):
    places = jnp.arange(segments.shape[0], dtype=jnp.int32)
    previous = jnp.concatenate([jnp.full((1,), -1, jnp.int32), segments[:-1]])
    starts = lax.cummax(jnp.where(segments != previous, places, 0), axis=0)
    return places - starts


def ring_order(n):
    return list(range(0, n, 2)) + list(range(n - 1, 0, -2))


def dp_gather(shard, n):
    if n != 8:
        return lax.all_gather(shard, "dp", axis=0, tiled=True)
    order = ring_order(n)
    place = {d: i for i, d in enumerate(order)}
    me = lax.axis_index("dp")
    rows = shard.shape[0]
    forth = [(order[i], order[(i + 1) % n]) for i in range(n)]
    back = [(order[(i + 1) % n], order[i]) for i in range(n)]

    def put(full, block, offset):
        table = jnp.array([order[(place[d] + offset) % n] for d in range(n)], jnp.int32)
        return lax.dynamic_update_slice_in_dim(full, block, table[me] * rows, 0)

    full = put(jnp.zeros((n * rows, shard.shape[1]), shard.dtype), shard, 0)
    ahead = behind = shard
    for s in range(1, n // 2 + 1):
        ahead = lax.ppermute(ahead, "dp", forth)
        full = put(full, ahead, -s)
        if s < n - n // 2:
            behind = lax.ppermute(behind, "dp", back)
            full = put(full, behind, s)
    return full


def dp_scatter(full, n, flip=False):
    if n != 8:
        return lax.psum_scatter(full, "dp", scatter_dimension=0, tiled=True).astype(F32)
    order = ring_order(n)
    if flip:
        order = order[::-1]
    place = {d: i for i, d in enumerate(order)}
    me = lax.axis_index("dp")
    rows = full.shape[0] // n
    forth = [(order[i], order[(i + 1) % n]) for i in range(n)]
    back = [(order[(i + 1) % n], order[i]) for i in range(n)]

    def part(offset):
        table = jnp.array([order[(place[d] + offset) % n] for d in range(n)], jnp.int32)
        return lax.dynamic_slice_in_dim(full, table[me] * rows, rows, 0)

    far = n // 2
    ahead = lax.ppermute(part(far), "dp", forth)
    behind = lax.ppermute(part(-(far - 1)), "dp", back)
    for s in range(1, far):
        ahead = lax.ppermute(ahead + part(far - s), "dp", forth)
        if s < far - 1:
            behind = lax.ppermute(behind + part(-(far - 1 - s)), "dp", back)
    return part(0).astype(F32) + ahead.astype(F32) + behind.astype(F32)


def per_device(
    n_dp,
    tokens,
    w_query,
    w_keyval,
    w_out,
    w_gate,
    w_up,
    w_down,
    norm_gains,
    segment_ids,
    grad_output,
):
    t = lax.axis_index("tensor").astype(jnp.int32)
    quarter, width = tokens.shape
    length = 4 * quarter
    q_cols = w_query.shape[1]
    units = w_gate.shape[1]

    def core(v):
        return lax.ppermute(v, "tensor", [(i, i ^ 1) for i in range(4)])

    def across(v):
        return lax.ppermute(v, "tensor", [(i, i ^ 2) for i in range(4)])

    def gather4(own):
        far = across(own)
        return own, core(own), far, core(far)

    def reduce4(own, other):
        half = own.shape[0] // 2
        chip = other[:half].astype(F32) + core(other[half:]).astype(F32)
        far = across(chip.astype(BF16))
        near = core(own[half:])
        return own[:half].astype(F32) + near.astype(F32) + far.astype(F32)

    gain_cols = jnp.pad(norm_gains.T, ((0, 0), (0, HEAD - 2)))
    attn_shard = jnp.concatenate([w_query, w_keyval, w_out.T, gain_cols], axis=1)
    ffn_shard = jnp.concatenate([w_gate, w_up, w_down.T], axis=1)
    attn_w = dp_gather(attn_shard, n_dp)
    ffn_shard, _ = lax.optimization_barrier((ffn_shard, attn_w))
    ffn_w = dp_gather(ffn_shard, n_dp)
    out_at = q_cols + 2 * HEAD
    w_out_t = attn_w[:, out_at : out_at + q_cols]
    gains = attn_w[:, out_at + q_cols : out_at + q_cols + 2].astype(F32).T
    gain_one_row, gain_two_row = gains[0:1], gains[1:2]
    w_gu, w_down_t = ffn_w[:, : 2 * units], ffn_w[:, 2 * units :]

    turn = t ^ jnp.arange(4, dtype=jnp.int32)
    positions = positions_of(segment_ids).reshape(4, quarter)[turn].reshape(length)
    valid = (segment_ids != 0).reshape(4, quarter)[turn].reshape(length).astype(F32)
    inverse = 10000.0 ** (-jnp.arange(HEAD // 2, dtype=F32) / (HEAD // 2))
    angles = positions.astype(F32)[:, None] * inverse[None, :]
    cos_half, sin_half = jnp.cos(angles), jnp.sin(angles)
    cos = jnp.concatenate([cos_half, cos_half], axis=1)
    sin = jnp.concatenate([-sin_half, sin_half], axis=1)
    pos3 = positions.reshape(length // BLK, 1, BLK)
    valid3 = valid.reshape(length // BLK, 1, BLK)
    t1 = t.reshape(1)

    parts = gather4(tokens)
    normed, q, k, v = project(parts, gain_one_row, attn_w, cos, sin, q_cols)
    half = length // 2
    mixed_far, lse_far = attention_forward(t1, q, k, v, pos3, valid3, half, half)
    mixed_near, lse_near = attention_forward(t1, q, k, v, pos3, valid3, 0, half)
    attn_far = dot_nt(mixed_far, w_out_t).astype(BF16)
    attn_near = dot_nt(mixed_near, w_out_t).astype(BF16)
    x_rows = tokens.astype(F32)
    residual = x_rows + reduce4(attn_near, attn_far)

    go = grad_output.astype(BF16)
    go, _ = lax.optimization_barrier((go, parts[2]))
    go_parts = gather4(go)
    go_near = jnp.concatenate(go_parts[:2])
    go_far = jnp.concatenate(go_parts[2:])
    gh_near = dot(go_near, w_down_t)
    gh_far = dot(go_far, w_down_t)

    scale_two = lax.rsqrt(jnp.mean(residual * residual, axis=-1, keepdims=True) + EPS)
    n2 = gather4((residual * scale_two * gain_two_row).astype(BF16))
    n2_near = jnp.concatenate(n2[:2])
    n2_far = jnp.concatenate(n2[2:])
    hidden_near, dgu_near = ffn_middle(n2_near, ffn_w, gh_near)
    hidden_far, dgu_far = ffn_middle(n2_far, ffn_w, gh_far)
    dn2_far = dot_nt(dgu_far, w_gu).astype(BF16)
    dn2_near = dot_nt(dgu_near, w_gu).astype(BF16)
    grad_n2 = reduce4(dn2_near, dn2_far)

    ffn_far = dot_nt(hidden_far, w_down_t).astype(BF16)
    ffn_near = dot_nt(hidden_near, w_down_t).astype(BF16)
    output = (residual + reduce4(ffn_near, ffn_far)).astype(BF16)

    dgu = jnp.concatenate([dgu_near, dgu_far])
    n2_all = jnp.concatenate([n2_near, n2_far])
    hidden = jnp.concatenate([hidden_near, hidden_far])
    go_all = jnp.concatenate([go_near, go_far])
    grad_w_gu = dot_tn(n2_all, dgu).astype(BF16)
    grad_w_down_t = dot_tn(go_all, hidden).astype(BF16)

    weighted = grad_n2 * gain_two_row
    inner = jnp.mean(residual * weighted, axis=-1, keepdims=True)
    grad_residual = grad_output + scale_two * weighted - residual * (scale_two**3 * inner)
    gain_two = jnp.sum(grad_n2 * residual * scale_two, axis=0)

    ga = jnp.concatenate(gather4(grad_residual.astype(BF16)))
    grad_mixed = (dot(ga, w_out_t) * valid[:, None]).astype(BF16)
    mixed = jnp.concatenate([mixed_near, mixed_far])
    lse = jnp.concatenate([lse_near, lse_far])
    dq, dkv = attention_backward(t1, q, grad_mixed, mixed, lse, k, v, pos3, cos, sin)
    dqkv = jnp.concatenate([dq, dkv], axis=1)
    w_qkv = attn_w[:, :out_at]
    dn_far = dot_nt(dqkv[half:], w_qkv).astype(BF16)
    dn_near = dot_nt(dqkv[:half], w_qkv).astype(BF16)
    grad_normed = reduce4(dn_near, dn_far)
    grad_w_out_t = dot_tn(ga, mixed).astype(BF16)
    grad_w_qkv = dot_tn(normed, dqkv).astype(BF16)

    scale_one = lax.rsqrt(jnp.mean(x_rows * x_rows, axis=-1, keepdims=True) + EPS)
    weighted = grad_normed * gain_one_row
    inner = jnp.mean(x_rows * weighted, axis=-1, keepdims=True)
    grad_tokens = grad_residual + scale_one * weighted - x_rows * (scale_one**3 * inner)
    gain_one = jnp.sum(grad_normed * x_rows * scale_one, axis=0)

    gu_shard = dp_scatter(grad_w_gu, n_dp)
    down_shard = dp_scatter(grad_w_down_t, n_dp, True)
    out_shard = dp_scatter(grad_w_out_t, n_dp, True)
    qkv_shard = dp_scatter(grad_w_qkv, n_dp)
    gain_cols = jnp.pad(jnp.stack([gain_one, gain_two], axis=1), ((0, 0), (0, HEAD - 2)))
    gain_shard = dp_scatter(gain_cols.astype(BF16), n_dp)
    small = jnp.concatenate([qkv_shard[:, q_cols:], gain_shard], axis=1)
    small = small + core(small)
    small = small + across(small)

    return (
        output,
        grad_tokens,
        qkv_shard[:, :q_cols],
        small[:, : 2 * HEAD],
        out_shard.T,
        gu_shard[:, :units],
        gu_shard[:, units:],
        down_shard.T,
        small[:, 2 * HEAD : 2 * HEAD + 2].T,
    )


def solution(mesh):
    return jax.shard_map(
        functools.partial(per_device, mesh.shape["dp"]),
        mesh=mesh,
        in_specs=(
            P(("dp", "tensor"), None),
            P("dp", "tensor"),
            P("dp", None),
            P("tensor", "dp"),
            P("dp", "tensor"),
            P("dp", "tensor"),
            P("tensor", "dp"),
            P(None, "dp"),
            P("dp"),
            P(("dp", "tensor"), None),
        ),
        out_specs=(
            P(("dp", "tensor"), None),
            P(("dp", "tensor"), None),
            P("dp", "tensor"),
            P("dp", None),
            P("tensor", "dp"),
            P("dp", "tensor"),
            P("dp", "tensor"),
            P("tensor", "dp"),
            P(None, "dp"),
        ),
        check_vma=False,
    )
```

time: 2010 us -> 587 us (0.29)
  waiting for transfers between devices: 1440 us -> 209 us
  matrix products: 300 us -> 112 us
  blocking collectives: 114 us -> 0 us
  Pallas kernels: 0 us -> 84.7 us
  starting transfers between devices: 1.34 us -> 65.4 us
  other arithmetic: 107 us -> 50.1 us
  local copies, waits for them, and re-layouts: 29.6 us -> 51.2 us
    reduce_scatter x10 -> x0, waiting for transfers between devices: 839 us -> none  [the longest x1 133 us: per_device(): lax.psum_scatter(grad_w_up, 'dp', scatter_dimension=0, tiled=True)]
    all_gather x14 -> x0, waiting for transfers between devices: 515 us -> none  [the longest x1 67.6 us: per_device(): lax.all_gather(again_shards[5], 'dp', axis=1, tiled=True)]
    ppermute x0 -> x75, waiting for transfers between devices: none -> 209 us  [the longest x9 87 us: across(): return lax.ppermute(v, 'tensor', [(i, i ^ 2) for i in range(4)])]
    dot_general x46 -> x15, matrix products: 300 us -> 112 us  [the longest x8 44.2 us: dot_nt(): return lax.dot_general(left, right, NT, preferred_element_type=F32)]
    all_gather x4 -> x0, blocking collectives: 108 us -> none  [the longest x1 35.2 us: per_device(): lax.all_gather(again_shards[1], 'dp', axis=0, tiled=True)]
    pallas_call x0 -> x6, Pallas kernels: none -> 84.7 us  [the longest x2 28.4 us: ffn_middle(): pl.pallas_call(ffn_kernel, grid=(rows // BLK,), in_specs=[row_spec(width)...]
    ppermute x0 -> x75, starting transfers between devices: none -> 65.4 us  [the longest x15 20.6 us: dp_scatter(): ahead = lax.ppermute(ahead + part(far - s), 'dp', forth)]
    unnamed x27 -> x0, waiting for transfers between devices: 48 us -> none
  transfers between devices with their start and end apart: 26 -> 75, of which waited for: 24 -> 21; matrix products, arithmetic and copies ran while one was open for 19% -> 35% of each run, Pallas kernels for 0% -> 15%
where the time goes in v1:
time: 587 us; the launch traced here: 580 us
  waiting for transfers between devices  209 us (36%)
  matrix products  112 us (19%)
  Pallas kernels  84.7 us (14%)
  starting transfers between devices  65.4 us (11%)
  local copies, waits for them, and re-layouts  51.2 us (9%)
  other arithmetic  50.1 us (9%)
  between operations  7 us (1%)
    ppermute x9, waiting for transfers between devices, across(): return lax.ppermute(v, 'tensor', [(i, i ^ 2) for i in range(4)])  87 us
    ppermute x8, waiting for transfers between devices, dp_gather(): ahead = lax.ppermute(ahead, 'dp', forth)  84.3 us
    dot_general x8, matrix products, dot_nt(): return lax.dot_general(left, right, NT, preferred_element_type=F32)  44.2 us
    dot_general x4, matrix products, dot_tn(): return lax.dot_general(left, right, TN, preferred_element_type=F32)  43.1 us
    pallas_call x2, Pallas kernels, ffn_middle(): pl.pallas_call(ffn_kernel, grid=(rows // BLK,), in_specs=[row_spec(width)...  28.4 us
    pallas_call x1, Pallas kernels, attention_backward(): pl.pallas_call(attn_bwd_kernel, grid_spec=pltpu.PrefetchScalarGridSpec(nu...  25.9 us
    dot_general x3, matrix products, dot(): return jnp.dot(left, right, preferred_element_type=F32)  24.9 us
    ppermute x15, starting transfers between devices, dp_scatter(): ahead = lax.ppermute(ahead + part(far - s), 'dp', forth)  20.6 us
  transfers between devices with their start and end apart: 75, of which 21 were waited for; matrix products, arithmetic and copies ran while one was open for 35% of the time, Pallas kernels for 15%

profile of v1, /device:TPU:0, one launch (start us, length us, event | category | flops | bytes accessed | tf_op | source)
XLA Modules:
  0.0 579.6 jit_solution(8710513994742658338)
XLA Ops:
  28.9 8.9 %collective-permute-done.5 = bf16[192,1152]{1,0:T(8,128)(2,1)S(1)} collective-permute-done((bf16[192,1152]{1,0:T(8,128)(2,1)S(1)}, bf16[192,1152]{1,0:T(8,128)(2,1)S(1)}, u32[]{:S(2)}, u32[]{:S(2)}) %collective-permute-start.5) | collective-permute-done | bytes 442400 | tf_op jit(solution)/shard_map/ppermute | solution.py:353
  41.5 8.2 %collective-permute-done.7 = bf16[192,1152]{1,0:T(8,128)(2,1)S(1)} collective-permute-done((bf16[192,1152]{1,0:T(8,128)(2,1)S(1)}, bf16[192,1152]{1,0:T(8,128)(2,1)S(1)}, u32[]{:S(2)}, u32[]{:S(2)}) %collective-permute-start.7) | collective-permute-done | bytes 442400 | tf_op jit(solution)/shard_map/ppermute | solution.py:353
  52.9 7.8 %collective-permute-done.9 = bf16[192,1152]{1,0:T(8,128)(2,1)S(1)} collective-permute-done((bf16[192,1152]{1,0:T(8,128)(2,1)S(1)}, bf16[192,1152]{1,0:T(8,128)(2,1)S(1)}, u32[]{:S(2)}, u32[]{:S(2)}) %collective-permute-start.9) | collective-permute-done | bytes 442400 | tf_op jit(solution)/shard_map/ppermute | solution.py:353
  72.2 5.0 broadcast_in_dim.10
  79.8 11.2 %collective-permute-done.14 = bf16[192,3456]{1,0:T(8,128)(2,1)} collective-permute-done((bf16[192,3456]{1,0:T(8,128)(2,1)}, bf16[192,3456]{1,0:T(8,128)(2,1)}, u32[]{:S(2)}, u32[]{:S(2)}) %collective-permute-start.14) | collective-permute-done | bytes 1327136 | tf_op jit(solution)/shard_map/ppermute | solution.py:353
  93.2 10.3 %project.1 = (bf16[2048,1536]{1,0:T(8,128)(2,1)S(1)}, bf16[2048,384]{1,0:T(8,128)(2,1)S(1)}, bf16[2048,128]{1,0:T(8,128)(2,1)S(1)}, bf16[2048,128]{1,0:T(8,128)(2,1)S(1)}) custom-call(bf16[512,1536]{1,0:T(8,128)(2,1)S(1)} %copy-done, bf16[512,1536]{1,0:T(8,128)(2,1)} %collective-permute-done.x1, bf16[512,1536]{1,0:T(8,128)(2,1)} %collective-permute-done.1.x2, ...), custom_call_target="tpu_custom_call" | custom-call | flops 4026531840 | bytes 12582912 | tf_op jit(solution)/shard_map/project/pallas_call | solution.py:75
  106.2 13.1 %attention_forward.3 = (bf16[1024,384]{1,0:T(8,128)(2,1)S(1)}, f32[4,1,768]{2,1,0:T(1,128)S(1)}) custom-call(s32[1]{0:T(128)} %bitcast.t_ref, bf16[2048,384]{1,0:T(8,128)(2,1)S(1)} %get-tuple-element.25.q, bf16[2048,128]{1,0:T(8,128)(2,1)S(1)} %get-tuple-element.26.k, bf16[2048,128]{1,0:T(8,128)(2,1)S(1)} %get-tuple-element.27.v, ...), custom_call_target="tpu_custom_call" | custom-call | flops 3221225472 | bytes 3145728 | tf_op jit(solution)/shard_map/attention_forward/pallas_call | solution.py:166
  124.4 7.0 %attention_forward.2 = (bf16[1024,384]{1,0:T(8,128)(2,1)S(1)}, f32[4,1,768]{2,1,0:T(1,128)S(1)}) custom-call(s32[1]{0:T(128)} %bitcast.t_ref, bf16[2048,384]{1,0:T(8,128)(2,1)S(1)} %get-tuple-element.25.q, bf16[2048,128]{1,0:T(8,128)(2,1)S(1)} %get-tuple-element.26.k, bf16[2048,128]{1,0:T(8,128)(2,1)S(1)} %get-tuple-element.27.v, ...), custom_call_target="tpu_custom_call" | custom-call | flops 3221225472 | bytes 3145728 | tf_op jit(solution)/shard_map/attention_forward/pallas_call | solution.py:166
  140.1 25.1 %collective-permute-done.18 = bf16[192,3456]{1,0:T(8,128)(2,1)S(1)} collective-permute-done((bf16[192,3456]{1,0:T(8,128)(2,1)}, bf16[192,3456]{1,0:T(8,128)(2,1)S(1)}, u32[]{:S(2)}, u32[]{:S(2)}) %collective-permute-start.18) | collective-permute-done | bytes 1327136 | tf_op jit(solution)/shard_map/ppermute | solution.py:353
  174.5 23.0 %collective-permute-done.20 = bf16[192,3456]{1,0:T(8,128)(2,1)} collective-permute-done((bf16[192,3456]{1,0:T(8,128)(2,1)S(1)}, bf16[192,3456]{1,0:T(8,128)(2,1)}, u32[]{:S(2)}, u32[]{:S(2)}) %collective-permute-start.20) | collective-permute-done | bytes 1327136 | tf_op jit(solution)/shard_map/ppermute | solution.py:353
  199.0 9.0 %fusion.35.grad_hidden = f32[1024,1152]{1,0:T(8,128)} fusion(bf16[512,1536]{1,0:T(8,128)(2,1)} %collective-permute-done.21, bf16[512,1536]{1,0:T(8,128)(2,1)S(1)} %copy-done.38, bf16[1536,3456]{1,0:T(8,128)(2,1)S(1)} %constant_dynamic-update-slice_fusion.w), kind=kOutput, calls=%fused_computation.49 | convolution fusion | flops 3630170112 | bytes 11403264 | tf_op jit(solution)/shard_map/dot_general | solution.py:25
  208.0 8.2 %fusion.39.grad_hidden = f32[1024,1152]{1,0:T(8,128)} fusion(bf16[512,1536]{1,0:T(8,128)(2,1)} %collective-permute-done.26, bf16[512,1536]{1,0:T(8,128)(2,1)} %collective-permute-done.25, bf16[1536,3456]{1,0:T(8,128)(2,1)S(1)} %constant_dynamic-update-slice_fusion.w), kind=kOutput, calls=%fused_computation.54 | convolution fusion | flops 3630170112 | bytes 11403264 | tf_op jit(solution)/shard_map/dot_general | solution.py:25
  218.5 14.3 %ffn_middle.2 = (bf16[1024,1152]{1,0:T(8,128)(2,1)S(1)}, bf16[1024,2304]{1,0:T(8,128)(2,1)}) custom-call(bf16[1024,1536]{1,0:T(8,128)(2,1)} %pad_maximum_fusion.1.n, bf16[1536,3456]{1,0:T(8,128)(2,1)} %copy-done.20, f32[1024,1152]{1,0:T(8,128)} %fusion.35.grad_hidden), custom_call_target="tpu_custom_call" | custom-call | flops 7247757312 | bytes 22020096 | tf_op jit(solution)/shard_map/ffn_middle/pallas_call | solution.py:308
  232.7 6.6 %convolution_convert_fusion.7 = bf16[1024,1536]{1,0:T(8,128)(2,1)S(1)} fusion(bf16[1024,1152]{1,0:T(8,128)(2,1)S(1)} %get-tuple-element.32, bf16[1536,3456]{1,0:T(8,128)(2,1)} %copy-done.20), kind=kOutput, calls=%fused_computation.41 | convolution fusion | flops 3625451520 | bytes 9043968 | tf_op jit(solution)/shard_map/dot_general | solution.py:29
  241.5 9.7 %fusion.24 = bf16[1024,1536]{1,0:T(8,128)(2,1)S(1)} fusion(bf16[1024,2304]{1,0:T(8,128)(2,1)S(1)} %copy-done.67, bf16[1536,3456]{1,0:T(8,128)(2,1)} %copy-done.20), kind=kOutput, calls=%fused_computation.36 | convolution fusion | flops 7249330176 | bytes 14942208 | tf_op jit(solution)/shard_map/dot_general | solution.py:29
  255.5 14.1 %ffn_middle.3 = (bf16[1024,1152]{1,0:T(8,128)(2,1)S(1)}, bf16[1024,2304]{1,0:T(8,128)(2,1)}) custom-call(bf16[1024,1536]{1,0:T(8,128)(2,1)} %pad_maximum_fusion.2.n, bf16[1536,3456]{1,0:T(8,128)(2,1)} %copy-done.20, f32[1024,1152]{1,0:T(8,128)} %fusion.39.grad_hidden), custom_call_target="tpu_custom_call" | custom-call | flops 7247757312 | bytes 22020096 | tf_op jit(solution)/shard_map/ffn_middle/pallas_call | solution.py:308
  269.6 6.6 %convolution_convert_fusion.6 = bf16[1024,1536]{1,0:T(8,128)(2,1)S(1)} fusion(bf16[1024,1152]{1,0:T(8,128)(2,1)S(1)} %get-tuple-element.33, bf16[1536,3456]{1,0:T(8,128)(2,1)} %copy-done.20), kind=kOutput, calls=%fused_computation.40 | convolution fusion | flops 3625451520 | bytes 9043968 | tf_op jit(solution)/shard_map/dot_general | solution.py:29
  276.2 11.4 %convolution_convert_fusion.1 = bf16[1536,1152]{1,0:T(8,128)(2,1)S(1)} fusion(bf16[512,1536]{1,0:T(8,128)(2,1)} %collective-permute-done.26, bf16[512,1536]{1,0:T(8,128)(2,1)} %collective-permute-done.25, bf16[512,1536]{1,0:T(8,128)(2,1)} %collective-permute-done.21, bf16[512,1536]{1,0:T(8,128)(2,1)S(1)} %copy-done.39, ...), kind=kOutput, calls=%fused_computation.6 | convolution fusion | flops 7284129792 | bytes 14548992 | tf_op jit(solution)/shard_map/dot_general | solution.py:33
  291.3 11.5 %fusion.27 = bf16[1024,1536]{1,0:T(8,128)(2,1)S(1)} fusion(bf16[1024,2304]{1,0:T(8,128)(2,1)} %get-tuple-element.35, bf16[1536,3456]{1,0:T(8,128)(2,1)} %copy-done.20), kind=kOutput, calls=%fused_computation.37 | convolution fusion | flops 7249330176 | bytes 14942208 | tf_op jit(solution)/shard_map/dot_general | solution.py:29
  305.5 21.7 %convolution_convert_fusion = bf16[1536,2304]{1,0:T(8,128)(2,1)} fusion(bf16[1024,2304]{1,0:T(8,128)(2,1)} %get-tuple-element.35, bf16[1024,2304]{1,0:T(8,128)(2,1)} %get-tuple-element.34, bf16[512,1536]{1,0:T(8,128)(2,1)} %copy-done.42, bf16[512,1536]{1,0:T(8,128)(2,1)} %copy-done.41, bf16[512,1536]{1,0:T(8,128)(2,1)} %copy-done.40, ...), kind=kOutput, calls=%fused_computation.2 | convolution fusion | flops 14543093760 | bytes 22806528 | tf_op jit(solution)/shard_map/dot_general | solution.py:33
  342.5 17.3 %collective-permute-done.72 = bf16[192,1152]{1,0:T(8,128)(2,1)S(1)} collective-permute-done((bf16[192,1152]{1,0:T(8,128)(2,1)S(1)}, bf16[192,1152]{1,0:T(8,128)(2,1)S(1)}, u32[]{:S(2)}, u32[]{:S(2)}) %collective-permute-start.72) | collective-permute-done | bytes 442400 | tf_op jit(solution)/shard_map/ppermute | solution.py:379
  363.7 8.9 %collective-permute-done.31 = bf16[512,1536]{1,0:T(8,128)(2,1)S(1)} collective-permute-done((bf16[512,1536]{1,0:T(8,128)(2,1)S(1)}, bf16[512,1536]{1,0:T(8,128)(2,1)S(1)}, u32[]{:S(2)}, u32[]{:S(2)}) %collective-permute-start.31) | collective-permute-done | bytes 1572896 | tf_op jit(solution)/shard_map/ppermute | solution.py:410
  376.1 28.4 %collective-permute-done.28 = bf16[512,1536]{1,0:T(8,128)(2,1)} collective-permute-done((bf16[512,1536]{1,0:T(8,128)(2,1)S(1)}, bf16[512,1536]{1,0:T(8,128)(2,1)}, u32[]{:S(2)}, u32[]{:S(2)}) %collective-permute-start.28) | collective-permute-done | bytes 1572896 | tf_op jit(solution)/shard_map/ppermute | solution.py:410
  404.5 5.1 fusion.73
  417.7 7.2 %collective-permute-done.71 = bf16[192,1152]{1,0:T(8,128)(2,1)S(1)} collective-permute-done((bf16[192,1152]{1,0:T(8,128)(2,1)S(1)}, bf16[192,1152]{1,0:T(8,128)(2,1)S(1)}, u32[]{:S(2)}, u32[]{:S(2)}) %collective-permute-start.71) | collective-permute-done | bytes 442400 | tf_op jit(solution)/shard_map/ppermute | solution.py:381
  424.9 19.4 %collective-permute-done.33 = bf16[512,1536]{1,0:T(8,128)(2,1)S(1)} collective-permute-done((bf16[512,1536]{1,0:T(8,128)(2,1)}, bf16[512,1536]{1,0:T(8,128)(2,1)S(1)}, u32[]{:S(2)}, u32[]{:S(2)}) %collective-permute-start.33) | collective-permute-done | bytes 1572896 | tf_op jit(solution)/shard_map/ppermute | solution.py:410
  451.0 7.7 %multiply_convert_fusion.do = bf16[2048,384]{1,0:T(8,128)(2,1)S(1)} fusion(f32[2048]{0:T(1024)S(1)} %bitcast.56, bf16[512,1536]{1,0:T(8,128)(2,1)} %copy-done.58, bf16[512,1536]{1,0:T(8,128)(2,1)S(1)} %collective-permute-done.33, bf16[512,1536]{1,0:T(8,128)(2,1)S(1)} %collective-permute-done.32, bf16[512,1536]{1,0:T(8,128)(2,1)} %get-tuple-element.74, ...), kind=kOutput, calls=%fused_computation.61 | convolution fusion | flops 2442657792 | bytes 9052160 | tf_op jit(solution)/shard_map/dot_general | solution.py:25
  458.7 25.9 %attention_backward.1 = (bf16[2048,384]{1,0:T(8,128)(2,1)S(1)}, bf16[2048,256]{1,0:T(8,128)(2,1)S(1)}) custom-call(s32[1]{0:T(128)} %bitcast.t_ref, bf16[2048,384]{1,0:T(8,128)(2,1)S(1)} %copy-done.11, bf16[2048,384]{1,0:T(8,128)(2,1)S(1)} %multiply_convert_fusion.do, bf16[2048,384]{1,0:T(8,128)(2,1)S(1)} %constant_dynamic-update-slice_fusion.16.mixed, ...), custom_call_target="tpu_custom_call" | custom-call | flops 16106127360 | bytes 9437184 | tf_op jit(solution)/shard_map/attention_backward/pallas_call | solution.py:252
  495.8 5.2 convolution_convert_fusion.8
  502.8 4.8 convolution_convert_fusion.9
  510.9 20.7 %collective-permute-done.37 = bf16[512,1536]{1,0:T(8,128)(2,1)S(1)} collective-permute-done((bf16[512,1536]{1,0:T(8,128)(2,1)S(1)}, bf16[512,1536]{1,0:T(8,128)(2,1)S(1)}, u32[]{:S(2)}, u32[]{:S(2)}) %collective-permute-start.37) | collective-permute-done | bytes 1572896 | tf_op jit(solution)/shard_map/ppermute | solution.py:410
  571.9 6.0 %collective-permute-done.53 = f32[192,384]{1,0:T(8,128)S(1)} collective-permute-done((f32[192,384]{1,0:T(8,128)S(1)}, f32[192,384]{1,0:T(8,128)S(1)}, u32[]{:S(2)}, u32[]{:S(2)}) %collective-permute-start.53) | collective-permute-done | bytes 294944 | tf_op jit(solution)/shard_map/ppermute | solution.py:410
  (416 shorter events, 183.1 us)
Async XLA Ops:
  5.9 47.1 %collective-permute-start.1 = (bf16[512,1536]{1,0:T(8,128)(2,1)S(1)}, bf16[512,1536]{1,0:T(8,128)(2,1)}, u32[]{:S(2)}, u32[]{:S(2)}) collective-permute-start(bf16[512,1536]{1,0:T(8,128)(2,1)S(1)} %copy-done), channel_id=1, source_target_pairs={{0,2},{1,3},{2,0},{3,1},{4,6},{5,7},{6,4},{7,5},{8,10},{9,11},{10,... | collective-permute-start | bytes 4718600 | tf_op jit(solution)/shard_map/ppermute | solution.py:410
  7.8 85.4 %collective-permute-start = (bf16[512,1536]{1,0:T(8,128)(2,1)S(1)}, bf16[512,1536]{1,0:T(8,128)(2,1)}, u32[]{:S(2)}, u32[]{:S(2)}) collective-permute-start(bf16[512,1536]{1,0:T(8,128)(2,1)S(1)} %copy-done), channel_id=1, source_target_pairs={{0,1},{1,0},{2,3},{3,2},{4,5},{5,4},{6,7},{7,6},{8,9},{9,8},{10,11... | collective-permute-start | bytes 4718600 | tf_op jit(solution)/shard_map/ppermute | solution.py:407
  52.9 40.2 %collective-permute-start.2 = (bf16[512,1536]{1,0:T(8,128)(2,1)}, bf16[512,1536]{1,0:T(8,128)(2,1)}, u32[]{:S(2)}, u32[]{:S(2)}) collective-permute-start(bf16[512,1536]{1,0:T(8,128)(2,1)} %collective-permute-done.1.x2), channel_id=1, source_target_pairs={{0,1},{1,0},{2,3},{3,2},{4,5},{5,4},{6,7},{7,6},{8,9},{9,8},{10,11... | collective-permute-start | bytes 4718600 | tf_op jit(solution)/shard_map/ppermute | solution.py:407
  67.4 72.5 %collective-permute-start.25 = (bf16[512,1536]{1,0:T(8,128)(2,1)}, bf16[512,1536]{1,0:T(8,128)(2,1)}, u32[]{:S(2)}, u32[]{:S(2)}) collective-permute-start(bf16[512,1536]{1,0:T(8,128)(2,1)} %convert_element_type.223), channel_id=1, source_target_pairs={{0,2},{1,3},{2,0},{3,1},{4,6},{5,7},{6,4},{7,5},{8,10},{9,11},{10,... | collective-permute-start | bytes 4718600 | tf_op jit(solution)/shard_map/ppermute | solution.py:410
  90.9 42.9 %collective-permute-start.16 = (bf16[192,3456]{1,0:T(8,128)(2,1)}, bf16[192,3456]{1,0:T(8,128)(2,1)}, u32[]{:S(2)}, u32[]{:S(2)}) collective-permute-start(bf16[192,3456]{1,0:T(8,128)(2,1)} %collective-permute-done.14), channel_id=1, source_target_pairs={{0,8},{8,16},{16,24},{24,28},{28,20},{20,12},{12,4},{4,0},{1,9},{9... | collective-permute-start | bytes 3981320 | tf_op jit(solution)/shard_map/ppermute | solution.py:353
  92.5 42.9 %collective-permute-start.17 = (bf16[192,3456]{1,0:T(8,128)(2,1)}, bf16[192,3456]{1,0:T(8,128)(2,1)}, u32[]{:S(2)}, u32[]{:S(2)}) collective-permute-start(bf16[192,3456]{1,0:T(8,128)(2,1)} %collective-permute-done.15), channel_id=1, source_target_pairs={{8,0},{16,8},{24,16},{28,24},{20,28},{12,20},{4,12},{0,4},{9,1},{1... | collective-permute-start | bytes 3981320 | tf_op jit(solution)/shard_map/ppermute | solution.py:356
  133.3 35.3 %collective-permute-start.10 = (bf16[512,1536]{1,0:T(8,128)(2,1)S(1)}, bf16[512,1536]{1,0:T(8,128)(2,1)S(1)}, u32[]{:S(2)}, u32[]{:S(2)}) collective-permute-start(bf16[512,1536]{1,0:T(8,128)(2,1)S(1)} %slice.147), channel_id=1, source_target_pairs={{0,1},{1,0},{2,3},{3,2},{4,5},{5,4},{6,7},{7,6},{8,9},{9,8},{10,11... | collective-permute-start | bytes 4718600 | tf_op jit(solution)/shard_map/ppermute | solution.py:407
  133.9 31.3 %collective-permute-start.18 = (bf16[192,3456]{1,0:T(8,128)(2,1)}, bf16[192,3456]{1,0:T(8,128)(2,1)S(1)}, u32[]{:S(2)}, u32[]{:S(2)}) collective-permute-start(bf16[192,3456]{1,0:T(8,128)(2,1)} %collective-permute-done.16), channel_id=1, source_target_pairs={{0,8},{8,16},{16,24},{24,28},{28,20},{20,12},{12,4},{4,0},{1,9},{9... | collective-permute-start | bytes 3981320 | tf_op jit(solution)/shard_map/ppermute | solution.py:353
  135.5 31.0 %collective-permute-start.19 = (bf16[192,3456]{1,0:T(8,128)(2,1)}, bf16[192,3456]{1,0:T(8,128)(2,1)S(1)}, u32[]{:S(2)}, u32[]{:S(2)}) collective-permute-start(bf16[192,3456]{1,0:T(8,128)(2,1)} %collective-permute-done.17), channel_id=1, source_target_pairs={{8,0},{16,8},{24,16},{28,24},{20,28},{12,20},{4,12},{0,4},{9,1},{1... | collective-permute-start | bytes 3981320 | tf_op jit(solution)/shard_map/ppermute | solution.py:356
  136.3 35.9 %collective-permute-start.12 = (bf16[512,1536]{1,0:T(8,128)(2,1)S(1)}, bf16[512,1536]{1,0:T(8,128)(2,1)S(1)}, u32[]{:S(2)}, u32[]{:S(2)}) collective-permute-start(bf16[512,1536]{1,0:T(8,128)(2,1)S(1)} %add_convert_fusion.4), channel_id=1, source_target_pairs={{0,2},{1,3},{2,0},{3,1},{4,6},{5,7},{6,4},{7,5},{8,10},{9,11},{10,... | collective-permute-start | bytes 4718600 | tf_op jit(solution)/shard_map/ppermute | solution.py:410
  140.0 59.0 %collective-permute-start.21 = (bf16[512,1536]{1,0:T(8,128)(2,1)S(1)}, bf16[512,1536]{1,0:T(8,128)(2,1)}, u32[]{:S(2)}, u32[]{:S(2)}) collective-permute-start(bf16[512,1536]{1,0:T(8,128)(2,1)S(1)} %copy-done.38), channel_id=1, source_target_pairs={{0,1},{1,0},{2,3},{3,2},{4,5},{5,4},{6,7},{7,6},{8,9},{9,8},{10,11... | collective-permute-start | bytes 4718600 | tf_op jit(solution)/shard_map/ppermute | solution.py:407
  165.2 42.8 %collective-permute-start.26 = (bf16[512,1536]{1,0:T(8,128)(2,1)}, bf16[512,1536]{1,0:T(8,128)(2,1)}, u32[]{:S(2)}, u32[]{:S(2)}) collective-permute-start(bf16[512,1536]{1,0:T(8,128)(2,1)} %collective-permute-done.25), channel_id=1, source_target_pairs={{0,1},{1,0},{2,3},{3,2},{4,5},{5,4},{6,7},{7,6},{8,9},{9,8},{10,11... | collective-permute-start | bytes 4718600 | tf_op jit(solution)/shard_map/ppermute | solution.py:407
  166.5 31.0 %collective-permute-start.20 = (bf16[192,3456]{1,0:T(8,128)(2,1)S(1)}, bf16[192,3456]{1,0:T(8,128)(2,1)}, u32[]{:S(2)}, u32[]{:S(2)}) collective-permute-start(bf16[192,3456]{1,0:T(8,128)(2,1)S(1)} %collective-permute-done.18), channel_id=1, source_target_pairs={{0,8},{8,16},{16,24},{24,28},{28,20},{20,12},{12,4},{4,0},{1,9},{9... | collective-permute-start | bytes 3981320 | tf_op jit(solution)/shard_map/ppermute | solution.py:353
  173.8 42.5 %collective-permute-start.13 = (bf16[512,1536]{1,0:T(8,128)(2,1)S(1)}, bf16[512,1536]{1,0:T(8,128)(2,1)S(1)}, u32[]{:S(2)}, u32[]{:S(2)}) collective-permute-start(bf16[512,1536]{1,0:T(8,128)(2,1)S(1)} %multiply_convert_fusion.1), channel_id=1, source_target_pairs={{0,1},{1,0},{2,3},{3,2},{4,5},{5,4},{6,7},{7,6},{8,9},{9,8},{10,11... | collective-permute-start | bytes 4718600 | tf_op jit(solution)/shard_map/ppermute | solution.py:407
  173.8 66.9 %collective-permute-start.23 = (bf16[512,1536]{1,0:T(8,128)(2,1)S(1)}, bf16[512,1536]{1,0:T(8,128)(2,1)S(1)}, u32[]{:S(2)}, u32[]{:S(2)}) collective-permute-start(bf16[512,1536]{1,0:T(8,128)(2,1)S(1)} %multiply_convert_fusion.1), channel_id=1, source_target_pairs={{0,2},{1,3},{2,0},{3,1},{4,6},{5,7},{6,4},{7,5},{8,10},{9,11},{10,... | collective-permute-start | bytes 4718600 | tf_op jit(solution)/shard_map/ppermute | solution.py:410
  252.6 110.6 %collective-permute-start.29 = (bf16[512,1536]{1,0:T(8,128)(2,1)}, bf16[512,1536]{1,0:T(8,128)(2,1)S(1)}, u32[]{:S(2)}, u32[]{:S(2)}) collective-permute-start(bf16[512,1536]{1,0:T(8,128)(2,1)} %slice.158), channel_id=1, source_target_pairs={{0,1},{1,0},{2,3},{3,2},{4,5},{5,4},{6,7},{7,6},{8,9},{9,8},{10,11... | collective-permute-start | bytes 4718600 | tf_op jit(solution)/shard_map/ppermute | solution.py:407
  288.5 40.7 %collective-permute-start.68 = (bf16[192,1152]{1,0:T(8,128)(2,1)}, bf16[192,1152]{1,0:T(8,128)(2,1)}, u32[]{:S(2)}, u32[]{:S(2)}) collective-permute-start(bf16[192,1152]{1,0:T(8,128)(2,1)} %constant_dynamic-slice_fusion.4), channel_id=1, source_target_pairs={{4,12},{12,20},{20,28},{28,24},{24,16},{16,8},{8,0},{0,4},{5,13},{... | collective-permute-start | bytes 1327112 | tf_op jit(solution)/shard_map/ppermute | solution.py:378
  291.3 43.9 %collective-permute-start.27 = (bf16[512,1536]{1,0:T(8,128)(2,1)}, bf16[512,1536]{1,0:T(8,128)(2,1)}, u32[]{:S(2)}, u32[]{:S(2)}) collective-permute-start(bf16[512,1536]{1,0:T(8,128)(2,1)} %slice.155), channel_id=1, source_target_pairs={{0,1},{1,0},{2,3},{3,2},{4,5},{5,4},{6,7},{7,6},{8,9},{9,8},{10,11... | collective-permute-start | bytes 4718600 | tf_op jit(solution)/shard_map/ppermute | solution.py:407
  328.6 32.6 %collective-permute-start.61 = (bf16[192,2304]{1,0:T(8,128)(2,1)S(1)}, bf16[192,2304]{1,0:T(8,128)(2,1)S(1)}, u32[]{:S(2)}, u32[]{:S(2)}) collective-permute-start(bf16[192,2304]{1,0:T(8,128)(2,1)S(1)} %constant_dynamic-slice_fusion.2), channel_id=1, source_target_pairs={{0,8},{8,16},{16,24},{24,28},{28,20},{20,12},{12,4},{4,0},{1,9},{9... | collective-permute-start | bytes 2654216 | tf_op jit(solution)/shard_map/ppermute | solution.py:378
  335.2 37.4 %collective-permute-start.31 = (bf16[512,1536]{1,0:T(8,128)(2,1)S(1)}, bf16[512,1536]{1,0:T(8,128)(2,1)S(1)}, u32[]{:S(2)}, u32[]{:S(2)}) collective-permute-start(bf16[512,1536]{1,0:T(8,128)(2,1)S(1)} %add_convert_fusion.1), channel_id=1, source_target_pairs={{0,2},{1,3},{2,0},{3,1},{4,6},{5,7},{6,4},{7,5},{8,10},{9,11},{10,... | collective-permute-start | bytes 4718600 | tf_op jit(solution)/shard_map/ppermute | solution.py:410
  342.5 33.0 %collective-permute-start.22 = (bf16[512,1536]{1,0:T(8,128)(2,1)S(1)}, bf16[512,1536]{1,0:T(8,128)(2,1)S(1)}, u32[]{:S(2)}, u32[]{:S(2)}) collective-permute-start(bf16[512,1536]{1,0:T(8,128)(2,1)S(1)} %copy-done.37), channel_id=1, source_target_pairs={{0,1},{1,0},{2,3},{3,2},{4,5},{5,4},{6,7},{7,6},{8,9},{9,8},{10,11... | collective-permute-start | bytes 4718600 | tf_op jit(solution)/shard_map/ppermute | solution.py:407
  359.7 44.7 %collective-permute-start.28 = (bf16[512,1536]{1,0:T(8,128)(2,1)S(1)}, bf16[512,1536]{1,0:T(8,128)(2,1)}, u32[]{:S(2)}, u32[]{:S(2)}) collective-permute-start(bf16[512,1536]{1,0:T(8,128)(2,1)S(1)} %add_convert_fusion.3), channel_id=1, source_target_pairs={{0,2},{1,3},{2,0},{3,1},{4,6},{5,7},{6,4},{7,5},{8,10},{9,11},{10,... | collective-permute-start | bytes 4718600 | tf_op jit(solution)/shard_map/ppermute | solution.py:410
  361.2 49.1 %collective-permute-start.70 = (bf16[192,1152]{1,0:T(8,128)(2,1)}, bf16[192,1152]{1,0:T(8,128)(2,1)}, u32[]{:S(2)}, u32[]{:S(2)}) collective-permute-start(bf16[192,1152]{1,0:T(8,128)(2,1)} %get-tuple-element.86), channel_id=1, source_target_pairs={{4,12},{12,20},{20,28},{28,24},{24,16},{16,8},{8,0},{0,4},{5,13},{... | collective-permute-start | bytes 1327112 | tf_op jit(solution)/shard_map/ppermute | solution.py:381
  363.2 47.1 %collective-permute-start.73 = (bf16[192,1152]{1,0:T(8,128)(2,1)S(1)}, bf16[192,1152]{1,0:T(8,128)(2,1)}, u32[]{:S(2)}, u32[]{:S(2)}) collective-permute-start(bf16[192,1152]{1,0:T(8,128)(2,1)S(1)} %get-tuple-element.87), channel_id=1, source_target_pairs={{12,4},{20,12},{28,20},{24,28},{16,24},{8,16},{0,8},{4,0},{13,5},{... | collective-permute-start | bytes 1327112 | tf_op jit(solution)/shard_map/ppermute | solution.py:383
  372.6 41.2 %collective-permute-start.62 = (bf16[192,2304]{1,0:T(8,128)(2,1)S(1)}, bf16[192,2304]{1,0:T(8,128)(2,1)S(1)}, u32[]{:S(2)}, u32[]{:S(2)}) collective-permute-start(bf16[192,2304]{1,0:T(8,128)(2,1)S(1)} %get-tuple-element.82), channel_id=1, source_target_pairs={{0,8},{8,16},{16,24},{24,28},{28,20},{20,12},{12,4},{4,0},{1,9},{9... | collective-permute-start | bytes 2654216 | tf_op jit(solution)/shard_map/ppermute | solution.py:381
  375.4 38.4 %collective-permute-start.65 = (bf16[192,2304]{1,0:T(8,128)(2,1)S(1)}, bf16[192,2304]{1,0:T(8,128)(2,1)}, u32[]{:S(2)}, u32[]{:S(2)}) collective-permute-start(bf16[192,2304]{1,0:T(8,128)(2,1)S(1)} %get-tuple-element.83), channel_id=1, source_target_pairs={{8,0},{16,8},{24,16},{28,24},{20,28},{12,20},{4,12},{0,4},{9,1},{1... | collective-permute-start | bytes 2654216 | tf_op jit(solution)/shard_map/ppermute | solution.py:379
  409.6 34.7 %collective-permute-start.33 = (bf16[512,1536]{1,0:T(8,128)(2,1)}, bf16[512,1536]{1,0:T(8,128)(2,1)S(1)}, u32[]{:S(2)}, u32[]{:S(2)}) collective-permute-start(bf16[512,1536]{1,0:T(8,128)(2,1)} %get-tuple-element.74), channel_id=1, source_target_pairs={{0,2},{1,3},{2,0},{3,1},{4,6},{5,7},{6,4},{7,5},{8,10},{9,11},{10,... | collective-permute-start | bytes 4718600 | tf_op jit(solution)/shard_map/ppermute | solution.py:410
  413.2 31.1 %collective-permute-start.74 = (bf16[192,1152]{1,0:T(8,128)(2,1)S(1)}, bf16[192,1152]{1,0:T(8,128)(2,1)S(1)}, u32[]{:S(2)}, u32[]{:S(2)}) collective-permute-start(bf16[192,1152]{1,0:T(8,128)(2,1)S(1)} %get-tuple-element.85), channel_id=1, source_target_pairs={{12,4},{20,12},{28,20},{24,28},{16,24},{8,16},{0,8},{4,0},{13,5},{... | collective-permute-start | bytes 1327112 | tf_op jit(solution)/shard_map/ppermute | solution.py:383
  447.3 40.7 %collective-permute-start.64 = (bf16[192,2304]{1,0:T(8,128)(2,1)}, bf16[192,2304]{1,0:T(8,128)(2,1)S(1)}, u32[]{:S(2)}, u32[]{:S(2)}) collective-permute-start(bf16[192,2304]{1,0:T(8,128)(2,1)} %get-tuple-element.78), channel_id=1, source_target_pairs={{0,8},{8,16},{16,24},{24,28},{28,20},{20,12},{12,4},{4,0},{1,9},{9... | collective-permute-start | bytes 2654216 | tf_op jit(solution)/shard_map/ppermute | solution.py:381
  449.0 39.0 %collective-permute-start.67 = (bf16[192,2304]{1,0:T(8,128)(2,1)}, bf16[192,2304]{1,0:T(8,128)(2,1)}, u32[]{:S(2)}, u32[]{:S(2)}) collective-permute-start(bf16[192,2304]{1,0:T(8,128)(2,1)} %get-tuple-element.79), channel_id=1, source_target_pairs={{8,0},{16,8},{24,16},{28,24},{20,28},{12,20},{4,12},{0,4},{9,1},{1... | collective-permute-start | bytes 2654216 | tf_op jit(solution)/shard_map/ppermute | solution.py:383
  495.2 36.4 %collective-permute-start.37 = (bf16[512,1536]{1,0:T(8,128)(2,1)S(1)}, bf16[512,1536]{1,0:T(8,128)(2,1)S(1)}, u32[]{:S(2)}, u32[]{:S(2)}) collective-permute-start(bf16[512,1536]{1,0:T(8,128)(2,1)S(1)} %add_convert_fusion), channel_id=1, source_target_pairs={{0,2},{1,3},{2,0},{3,1},{4,6},{5,7},{6,4},{7,5},{8,10},{9,11},{10,... | collective-permute-start | bytes 4718600 | tf_op jit(solution)/shard_map/ppermute | solution.py:410
  508.8 31.0 %collective-permute-start.39 = (bf16[192,640]{1,0:T(8,128)(2,1)S(1)}, bf16[192,640]{1,0:T(8,128)(2,1)S(1)}, u32[]{:S(2)}, u32[]{:S(2)}) collective-permute-start(bf16[192,640]{1,0:T(8,128)(2,1)S(1)} %get-tuple-element.95), channel_id=1, source_target_pairs={{0,8},{8,16},{16,24},{24,28},{28,20},{20,12},{12,4},{4,0},{1,9},{9... | collective-permute-start | bytes 737288 | tf_op jit(solution)/shard_map/ppermute | solution.py:381
  (118 other events, 1516.1 us)

commit v2 on v1

--- a/solution.py
+++ b/solution.py
@@ -33,97 +33,41 @@
     return lax.dot_general(left, right, TN, preferred_element_type=F32)
 
 
-def qkv_kernel(x0, x1, x2, x3, gain, w, cos, sin, normed, q, k, v, held):
-    i = pl.program_id(0)
-    per = pl.num_programs(0) // 4
-    for j, ref in enumerate((x0, x1, x2, x3)):
-
-        @pl.when(i // per == j)
-        def _(ref=ref):
-            held[...] = ref[...]
-
-    rows = held[...].astype(F32)
-    scale = lax.rsqrt(jnp.mean(rows * rows, axis=-1, keepdims=True) + EPS)
-    n = (rows * scale * gain[...]).astype(BF16)
-    normed[...] = n
-    y = dot(n, w[...])
-    c, s = cos[...], sin[...]
-    heads = q.shape[1] // HEAD
-
-    def turned(a):
-        return (a * c + pltpu.roll(a, HEAD // 2, 1) * s).astype(BF16)
-
-    for h in range(heads):
-        q[:, h * HEAD : (h + 1) * HEAD] = turned(y[:, h * HEAD : (h + 1) * HEAD])
-    at = heads * HEAD
-    k[...] = turned(y[:, at : at + HEAD])
-    v[...] = y[:, at + HEAD : at + 2 * HEAD].astype(BF16)
-
-
-def project(parts, gain, weights, cos, sin, q_cols):
-    quarter, width = parts[0].shape
-    rows = 4 * quarter
-    per = quarter // BLK
-    cols = q_cols + 2 * HEAD
-
-    def part_spec(j):
-        return pl.BlockSpec((BLK, width), lambda i: (jnp.clip(i - j * per, 0, per - 1), 0))
-
-    def row_spec(n):
-        return pl.BlockSpec((BLK, n), lambda i: (i, 0))
-
-    return pl.pallas_call(
-        qkv_kernel,
-        grid=(rows // BLK,),
-        in_specs=[part_spec(j) for j in range(4)]
-        + [
-            pl.BlockSpec((1, width), lambda i: (0, 0)),
-            pl.BlockSpec((width, cols), lambda i: (0, 0)),
-            row_spec(HEAD),
-            row_spec(HEAD),
-        ],
-        out_specs=[row_spec(width), row_spec(q_cols), row_spec(HEAD), row_spec(HEAD)],
-        out_shape=[
-            jax.ShapeDtypeStruct((rows, width), BF16),
-            jax.ShapeDtypeStruct((rows, q_cols), BF16),
-            jax.ShapeDtypeStruct((rows, HEAD), BF16),
-            jax.ShapeDtypeStruct((rows, HEAD), BF16),
-        ],
-        scratch_shapes=[pltpu.VMEM((BLK, width), BF16)],
-        compiler_params=pltpu.CompilerParams(vmem_limit_bytes=32 * MIB),
-        cost_estimate=pl.CostEstimate(
-            flops=2 * rows * width * cols, bytes_accessed=4 * rows * width, transcendentals=0
-        ),
-        name="project",
-    )(*parts, gain, weights, cos, sin)
-
-
 def stacked(block, heads):
     return jnp.concatenate([block[:, h * HEAD : (h + 1) * HEAD] for h in range(heads)], axis=0)
 
 
+def partner(t, j):
+    rem, div = lax.rem, lax.div
+    two = jnp.int32(2)
+    j = jnp.int32(j)
+    return rem(div(t, two) + div(j, two), two) * 2 + rem(rem(t, two) + rem(j, two), two)
+
+
 def key_row(t, kb):
     per = 512 // BLK
-    return pl.multiple_of(((t ^ (kb // per)) * per + kb % per) * BLK, BLK)
+    return pl.multiple_of((partner(t, lax.div(kb, per)) * per + lax.rem(kb, per)) * BLK, BLK)
 
 
 def query_block(t, i):
     per = 512 // BLK
-    return (t ^ (i // per)) * per + i % per
+    i = jnp.int32(i)
+    return partner(t, lax.div(i, per)) * per + lax.rem(i, per)
 
 
 def tiled3(row, heads):
     return jnp.concatenate([row] * heads, axis=1)
 
 
-def attn_fwd_kernel(first, t_ref, q, k, v, pos, valid, mixed, lse):
-    heads = q.shape[1] // HEAD
+def attend(t, i, q, k, v, pos, valid, mixed, lse):
+    cols = q.shape[1]
+    heads = cols // HEAD
     wide = heads * BLK
-    t = t_ref[0]
-    qb = query_block(t, pl.program_id(0) + first)
-    q3 = stacked(q[...], heads)
+    qb = query_block(t, i)
+    mine = pl.ds(pl.multiple_of(i * BLK, BLK), BLK)
+    q3 = stacked(q[mine, :], heads)
     at = qb * BLK + lax.broadcasted_iota(jnp.int32, (1, BLK), 1)
-    low = at - jnp.minimum(pos[0], WINDOW - 1)
+    low = at - jnp.minimum(pos[i], WINDOW - 1)
     at3, low3 = tiled3(at, heads), tiled3(low, heads)
     factor = HEAD**-0.5 * LOG2E
 
@@ -150,46 +94,380 @@
             jnp.zeros((HEAD, wide), F32),
         ),
     )
-    lse[0] = peak + jnp.log2(total)
-    acc = acc * (tiled3(valid[0], heads) / total)
-    for h in range(heads):
-        mixed[:, h * HEAD : (h + 1) * HEAD] = acc[:, h * BLK : (h + 1) * BLK].T.astype(BF16)
-
-
-def attention_forward(t, q, k, v, pos, valid, first_row, rows):
-    cols = q.shape[1]
-    heads = cols // HEAD
-    first = first_row // BLK
-    blocks = rows // BLK
-    full = pl.BlockSpec((k.shape[0], HEAD), lambda i, t: (0, 0))
-    lane = pl.BlockSpec((1, 1, BLK), lambda i, t: (i + first, 0, 0))
+    lse[i] = peak + jnp.log2(total)
+    acc = acc * (tiled3(valid[i], heads) / total)
+    mixed[mine, :] = jnp.concatenate(
+        [acc[:, h * BLK : (h + 1) * BLK].T for h in range(heads)], axis=1
+    ).astype(BF16)
+
+
+def ring_device(p, n):
+    p = lax.rem(p + n, jnp.int32(n))
+    down = lax.div(p, jnp.int32(n // 2))
+    return (1 - down) * 2 * p + down * (2 * (n - 1 - p) + 1)
+
+
+def ring_place(d, n):
+    z, y = lax.div(d, jnp.int32(2)), lax.rem(d, jnp.int32(2))
+    return z + y * (n - 1 - 2 * z)
+
+
+def send(src, dst, sems, at, device):
+    return pltpu.make_async_remote_copy(
+        src_ref=src,
+        dst_ref=dst,
+        send_sem=sems.at[0, at],
+        recv_sem=sems.at[1, at],
+        device_id=device,
+        device_id_type=pl.DeviceIdType.MESH,
+    )
+
+
+class Ring:
+    def __init__(self, shard, full, sems, first_sem, own, n, direction):
+        self.shard, self.full, self.sems, self.at, self.own = shard, full, sems, first_sem, own
+        self.n, self.dir = n, direction
+        self.copies = {}
+
+    def block(self, offset, place):
+        rows = self.shard.shape[0]
+        at = ring_device(place + offset * self.dir, self.n) * rows
+        return self.full.at[pl.ds(pl.multiple_of(at, rows & -rows), rows), :]
+
+    def begin(self, place):
+        self.place = place
+        if self.n == 8:
+            target = self.block(0, place)
+        else:
+            target = self.full
+        self.local = pltpu.make_async_copy(self.shard, target, self.own)
+        self.local.start()
+        self.start(1)
+
+    def start(self, s):
+        if self.n != 8:
+            return
+        for way in (0, 1):
+            if s > self.n // 2 - way:
+                continue
+            sign = 1 - 2 * way
+            block = self.block(-sign * (s - 1), self.place)
+            device = ring_device(self.place + sign * self.dir, self.n)
+            src = self.shard if s == 1 else block
+            at = self.at + 2 * (s - 1) + way
+            copy = send(src, block, self.sems, at, {"dp": device})
+            copy.start()
+            self.copies[s, way] = copy
+
+    def arrived(self, s):
+        for way in (0, 1):
+            if (s, way) in self.copies:
+                self.copies[s, way].wait_recv()
+
+    def next(self, s):
+        self.arrived(s)
+        self.start(s + 1)
+
+    def end(self):
+        for copy in self.copies.values():
+            copy.wait_send()
+        self.local.wait()
+
+
+def front_kernel(
+    n_dp,
+    tokens,
+    grad_output,
+    shard_a,
+    shard_d,
+    shard_g,
+    pos,
+    valid,
+    cos,
+    sin,
+    w_a_out,
+    w_d_out,
+    w_g,
+    gains,
+    normed_out,
+    q_out,
+    k_out,
+    v_out,
+    mixed_out,
+    lse,
+    residual_out,
+    n2_out,
+    go_out,
+    gh_out,
+    w_a,
+    w_d,
+    x4,
+    normed,
+    q,
+    k,
+    v,
+    mixed,
+    near_recv,
+    far_recv,
+    x_recv,
+    sum_buf,
+    n2_own,
+    go_buf,
+    gh_buf,
+    res,
+    ring_sems,
+    pair_sems,
+    local_sems,
+):
+    quarter, width = tokens.shape
+    q_cols = q.shape[1]
+    heads = q_cols // HEAD
+    kv_at = q_cols + 2 * HEAD
+    gain_at = kv_at + q_cols
+    t = lax.axis_index("tensor").astype(jnp.int32)
+    place = ring_place(lax.axis_index("dp").astype(jnp.int32), n_dp)
+    near_id, far_id = {"tensor": partner(t, 1)}, {"tensor": partner(t, 2)}
+
+    barrier = pltpu.get_barrier_semaphore()
+    partners = [near_id, far_id]
+    if n_dp == 8:
+        partners += [{"dp": ring_device(place + 1, n_dp)}, {"dp": ring_device(place - 1, n_dp)}]
+    for device in partners:
+        pl.semaphore_signal(barrier, inc=1, device_id=device, device_id_type=pl.DeviceIdType.MESH)
+    pl.semaphore_wait(barrier, len(partners))
+
+    def rows_of(ref, j, size=1):
+        return ref.at[pl.ds(j * quarter, size * quarter), :]
+
+    used = [0]
+
+    def local(src, dst):
+        copy = pltpu.make_async_copy(src, dst, local_sems.at[used[0]])
+        used[0] += 1
+        copy.start()
+        return copy
+
+    ring_a = Ring(shard_a, w_a, ring_sems, 0, local_sems.at[24], n_dp, 1)
+    ring_d = Ring(shard_d, w_d, ring_sems, 8, local_sems.at[25], n_dp, 1)
+    ring_g = Ring(shard_g, w_g, ring_sems, 16, local_sems.at[26], n_dp, -1)
+
+    ring_a.begin(place)
+    x_far = send(tokens, rows_of(x4, 2), pair_sems, 0, far_id)
+    x_far.start()
+    x_near = send(tokens, rows_of(x4, 1), pair_sems, 1, near_id)
+    x_near.start()
+    x_own = local(tokens, rows_of(x4, 0))
+    go_in = local(grad_output, res)
+    for s in (1, 2, 3):
+        ring_a.next(s)
+    ring_d.begin(place)
+    ring_g.begin(place)
+    ring_a.arrived(4)
+    ring_a.local.wait()
+
+    gain_rows = w_a[:, gain_at : gain_at + HEAD].astype(F32).T
+    gains[...] = gain_rows[:8]
+
+    def project(i, carry):
+        mine = pl.ds(pl.multiple_of(i * BLK, BLK), BLK)
+        rows = x4[mine, :].astype(F32)
+        scale = lax.rsqrt(jnp.mean(rows * rows, axis=-1, keepdims=True) + EPS)
+        n = (rows * scale * gains[0:1, :]).astype(BF16)
+        normed[mine, :] = n
+        y = dot(n, w_a[:, :kv_at])
+        c, s = cos[mine, :], sin[mine, :]
+
+        def turned(a):
+            return (a * c + pltpu.roll(a, HEAD // 2, 1) * s).astype(BF16)
+
+        q[mine, :] = jnp.concatenate(
+            [turned(y[:, h * HEAD : (h + 1) * HEAD]) for h in range(heads)], axis=1
+        )
+        k[mine, :] = turned(y[:, q_cols : q_cols + HEAD])
+        v[mine, :] = y[:, q_cols + HEAD : kv_at].astype(BF16)
+        return carry
+
+    per = quarter // BLK
+    x_own.wait()
+    x_near.wait_recv()
+    lax.fori_loop(0, 2 * per, project, 0)
+    x_far.wait_recv()
+    x_last = send(rows_of(x4, 2), rows_of(x4, 3), pair_sems, 2, near_id)
+    x_last.start()
+    go_in.wait()
+    go_buf[...] = res[...].astype(BF16)
+    go_far = send(go_buf, rows_of(go_out, 2), pair_sems, 3, far_id)
+    go_far.start()
+    go_near = send(go_buf, rows_of(go_out, 1), pair_sems, 4, near_id)
+    go_near.start()
+    go_own = local(go_buf, rows_of(go_out, 0))
+    x_last.wait_recv()
+    lax.fori_loop(2 * per, 4 * per, project, 0)
+    copies = [
+        local(normed, normed_out),
+        local(q, q_out),
+        local(k, k_out),
+        local(v, v_out),
+        local(w_a, w_a_out),
+    ]
+
+    def attention(i, carry):
+        attend(t, i, q, k, v, pos, valid, mixed, lse)
+        return carry
+
+    part = x4
+
+    def out_product(i, carry):
+        mine = pl.ds(pl.multiple_of(i * BLK, BLK), BLK)
+        part[mine, :] = dot_nt(mixed[mine, :], w_a[:, kv_at:gain_at]).astype(BF16)
+        return carry
+
+    x_last.wait_send()
+    lax.fori_loop(2 * per, 4 * per, attention, 0)
+    ring_d.next(1)
+    lax.fori_loop(2 * per, 4 * per, out_product, 0)
+    part_far = send(rows_of(part, 3), far_recv, pair_sems, 5, near_id)
+    part_far.start()
+    lax.fori_loop(0, 1, attention, 0)
+    part_far.wait_recv()
+    sum_buf[...] = (part[pl.ds(2 * quarter, quarter), :].astype(F32) + far_recv[...].astype(F32)).astype(BF16)
+    sum_far = send(sum_buf, x_recv, pair_sems, 6, far_id)
+    sum_far.start()
+    ring_g.next(1)
+    lax.fori_loop(1, 2 * per, attention, 0)
+    lax.fori_loop(0, 2 * per, out_product, 0)
+    part_near = send(rows_of(part, 1), near_recv, pair_sems, 7, near_id)
+    part_near.start()
+    copies.append(local(mixed, mixed_out))
+    ring_d.next(2)
+    ring_d.next(3)
+    ring_g.next(2)
+    go_far.wait_recv()
+    go_last = send(rows_of(go_out, 2), rows_of(go_out, 3), pair_sems, 8, near_id)
+    go_last.start()
+    part_near.wait_recv()
+    sum_far.wait_recv()
+
+    res[...] = (
+        tokens[...].astype(F32)
+        + part[pl.ds(0, quarter), :].astype(F32)
+        + near_recv[...].astype(F32)
+        + x_recv[...].astype(F32)
+    )
+    scale_two = lax.rsqrt(jnp.mean(res[...] * res[...], axis=-1, keepdims=True) + EPS)
+    n2_own[...] = (res[...] * scale_two * gains[1:2, :]).astype(BF16)
+    n2_far = send(n2_own, rows_of(n2_out, 2), pair_sems, 9, far_id)
+    n2_far.start()
+    n2_near = send(n2_own, rows_of(n2_out, 1), pair_sems, 10, near_id)
+    n2_near.start()
+    copies.append(local(n2_own, rows_of(n2_out, 0)))
+    copies.append(local(res, residual_out))
+
+    ring_d.arrived(4)
+    ring_d.local.wait()
+    copies.append(local(w_d, w_d_out))
+    go_far.wait_send()
+    go_near.wait_send()
+    go_own.wait()
+
+    def grad_hidden(i, carry):
+        mine = pl.ds(pl.multiple_of(i * BLK, BLK), BLK)
+        gh_buf[mine, :] = dot(go_buf[mine, :], w_d[...]).astype(BF16)
+        return carry
+
+    for j in range(4):
+        if j == 1:
+            go_near.wait_recv()
+        if j == 3:
+            go_last.wait_recv()
+        if j > 0:
+            load = local(rows_of(go_out, j), go_buf)
+            load.wait()
+        if j > 0:
+            store.wait()
+        lax.fori_loop(0, per, grad_hidden, 0)
+        store = local(gh_buf, rows_of(gh_out, j))
+        if j == 1:
+            ring_g.next(3)
+
+    n2_far.wait_recv()
+    n2_last = send(rows_of(n2_out, 2), rows_of(n2_out, 3), pair_sems, 11, near_id)
+    n2_last.start()
+    ring_g.arrived(4)
+    store.wait()
+    for copy in copies:
+        copy.wait()
+    for copy in (x_far, x_near, part_far, sum_far, part_near, go_last, n2_far, n2_near, n2_last):
+        copy.wait_send()
+    n2_near.wait_recv()
+    n2_last.wait_recv()
+    ring_a.copies and [c.wait_send() for c in ring_a.copies.values()]
+    ring_d.copies and [c.wait_send() for c in ring_d.copies.values()]
+    ring_g.end()
+
+
+def front(n_dp, tokens, grad_output, shard_a, shard_d, shard_g, pos, valid, cos, sin, q_cols):
+    quarter, width = tokens.shape
+    length = 4 * quarter
+    heads = q_cols // HEAD
+    units = shard_d.shape[1]
+    cols_a = shard_a.shape[1]
+    vmem = pl.BlockSpec(memory_space=pltpu.VMEM)
+    hbm = pl.BlockSpec(memory_space=pl.ANY)
+    blocks = length // BLK
+
+    def out(rows, cols, kind=BF16):
+        return jax.ShapeDtypeStruct((rows, cols), kind)
+
     return pl.pallas_call(
-        functools.partial(attn_fwd_kernel, first),
-        grid_spec=pltpu.PrefetchScalarGridSpec(
-            num_scalar_prefetch=1,
-            grid=(blocks,),
-            in_specs=[
-                pl.BlockSpec((BLK, cols), lambda i, t: (i + first, 0)),
-                full,
-                full,
-                lane,
-                lane,
-            ],
-            out_specs=[
-                pl.BlockSpec((BLK, cols), lambda i, t: (i, 0)),
-                pl.BlockSpec((1, 1, heads * BLK), lambda i, t: (i, 0, 0)),
-            ],
+        functools.partial(front_kernel, n_dp),
+        in_specs=[vmem, hbm, hbm, hbm, hbm, vmem, vmem, vmem, vmem],
+        out_specs=[hbm, hbm, hbm, vmem, hbm, hbm, hbm, hbm, hbm, vmem, hbm, hbm, hbm, hbm],
+        out_shape=[
+            out(width, cols_a),
+            out(width, units),
+            out(width, 2 * units),
+            out(8, width, F32),
+            out(length, width),
+            out(length, q_cols),
+            out(length, HEAD),
+            out(length, HEAD),
+            out(length, q_cols),
+            jax.ShapeDtypeStruct((blocks, 1, heads * BLK), F32),
+            out(quarter, width, F32),
+            out(length, width),
+            out(length, width),
+            out(length, units),
+        ],
+        scratch_shapes=[
+            pltpu.VMEM((width, cols_a), BF16),
+            pltpu.VMEM((width, units), BF16),
+            pltpu.VMEM((length, width), BF16),
+            pltpu.VMEM((length, width), BF16),
+            pltpu.VMEM((length, q_cols), BF16),
+            pltpu.VMEM((length, HEAD), BF16),
+            pltpu.VMEM((length, HEAD), BF16),
+            pltpu.VMEM((length, q_cols), BF16),
+            pltpu.VMEM((quarter, width), BF16),
+            pltpu.VMEM((quarter, width), BF16),
+            pltpu.VMEM((quarter, width), BF16),
+            pltpu.VMEM((quarter, width), BF16),
+            pltpu.VMEM((quarter, width), BF16),
+            pltpu.VMEM((quarter, width), BF16),
+            pltpu.VMEM((quarter, units), BF16),
+            pltpu.VMEM((quarter, width), F32),
+            pltpu.SemaphoreType.DMA((2, 24)),
+            pltpu.SemaphoreType.DMA((2, 12)),
+            pltpu.SemaphoreType.DMA((32,)),
+        ],
+        compiler_params=pltpu.CompilerParams(
+            collective_id=0, has_side_effects=True, vmem_limit_bytes=58 * MIB
         ),
-        out_shape=[
-            jax.ShapeDtypeStruct((rows, cols), BF16),
-            jax.ShapeDtypeStruct((blocks, 1, heads * BLK), F32),
-        ],
-        compiler_params=pltpu.CompilerParams(vmem_limit_bytes=32 * MIB),
         cost_estimate=pl.CostEstimate(
-            flops=8 * rows * WINDOW * cols, bytes_accessed=8 * rows * cols, transcendentals=rows * WINDOW * heads
+            flops=12 * length * width * q_cols, bytes_accessed=64 * MIB, transcendentals=0
         ),
-        name="attention_forward",
-    )(t, q, k, v, pos, valid)
+        name="front",
+    )(tokens, grad_output, shard_a, shard_d, shard_g, pos, valid, cos, sin)
 
 
 def attn_bwd_kernel(t_ref, q, do, mixed, lse, k, v, pos, cos, sin, cos_all, sin_all, dq, dkv, dk_acc, dv_acc):
@@ -286,7 +564,7 @@
     half = hidden.shape[1]
     y = dot(n[...], w[...])
     gate, up = y[:, :half], y[:, half:]
-    gh = grad_hidden[...]
+    gh = grad_hidden[...].astype(F32)
     root = (2.0 / jnp.pi) ** 0.5
     square = gate * gate
     th = jnp.tanh(root * gate * (1.0 + 0.044715 * square))
@@ -298,28 +576,34 @@
     grads[:, half:] = (gh * act).astype(BF16)
 
 
-def ffn_middle(n, w, grad_hidden):
-    rows, width = n.shape
+def ffn_middle(n, w, grad_hidden, first_row, rows, earlier):
+    length, width = n.shape
     half = grad_hidden.shape[1]
+    first = first_row // BLK
 
     def row_spec(c):
-        return pl.BlockSpec((BLK, c), lambda i: (i, 0))
+        return pl.BlockSpec((BLK, c), lambda i: (i + first, 0))
+
+    def body(n_ref, w_ref, gh_ref, *refs):
+        ffn_kernel(n_ref, w_ref, gh_ref, *refs[-2:])
 
     return pl.pallas_call(
-        ffn_kernel,
+        body,
         grid=(rows // BLK,),
-        in_specs=[row_spec(width), pl.BlockSpec((width, 2 * half), lambda i: (0, 0)), row_spec(half)],
+        in_specs=[row_spec(width), pl.BlockSpec((width, 2 * half), lambda i: (0, 0)), row_spec(half)]
+        + [pl.BlockSpec(memory_space=pl.ANY)] * len(earlier),
         out_specs=[row_spec(half), row_spec(2 * half)],
         out_shape=[
-            jax.ShapeDtypeStruct((rows, half), BF16),
-            jax.ShapeDtypeStruct((rows, 2 * half), BF16),
+            jax.ShapeDtypeStruct((length, half), BF16),
+            jax.ShapeDtypeStruct((length, 2 * half), BF16),
         ],
+        input_output_aliases={3: 0, 4: 1} if earlier else {},
         compiler_params=pltpu.CompilerParams(vmem_limit_bytes=50 * MIB),
         cost_estimate=pl.CostEstimate(
             flops=4 * rows * width * half, bytes_accessed=14 * rows * width, transcendentals=rows * half
         ),
         name="ffn_middle",
-    )(n, w, grad_hidden)
+    )(n, w, grad_hidden, *earlier)
 
 
 def positions_of(segments):
@@ -331,31 +615,6 @@
 
 def ring_order(n):
     return list(range(0, n, 2)) + list(range(n - 1, 0, -2))
-
-
-def dp_gather(shard, n):
-    if n != 8:
-        return lax.all_gather(shard, "dp", axis=0, tiled=True)
-    order = ring_order(n)
-    place = {d: i for i, d in enumerate(order)}
-    me = lax.axis_index("dp")
-    rows = shard.shape[0]
-    forth = [(order[i], order[(i + 1) % n]) for i in range(n)]
-    back = [(order[(i + 1) % n], order[i]) for i in range(n)]
-
-    def put(full, block, offset):
-        table = jnp.array([order[(place[d] + offset) % n] for d in range(n)], jnp.int32)
-        return lax.dynamic_update_slice_in_dim(full, block, table[me] * rows, 0)
-
-    full = put(jnp.zeros((n * rows, shard.shape[1]), shard.dtype), shard, 0)
-    ahead = behind = shard
-    for s in range(1, n // 2 + 1):
-        ahead = lax.ppermute(ahead, "dp", forth)
-        full = put(full, ahead, -s)
-        if s < n - n // 2:
-            behind = lax.ppermute(behind, "dp", back)
-            full = put(full, behind, s)
-    return full
 
 
 def dp_scatter(full, n, flip=False):
@@ -421,16 +680,13 @@
         return own[:half].astype(F32) + near.astype(F32) + far.astype(F32)
 
     gain_cols = jnp.pad(norm_gains.T, ((0, 0), (0, HEAD - 2)))
-    attn_shard = jnp.concatenate([w_query, w_keyval, w_out.T, gain_cols], axis=1)
-    ffn_shard = jnp.concatenate([w_gate, w_up, w_down.T], axis=1)
-    attn_w = dp_gather(attn_shard, n_dp)
-    ffn_shard, _ = lax.optimization_barrier((ffn_shard, attn_w))
-    ffn_w = dp_gather(ffn_shard, n_dp)
-    out_at = q_cols + 2 * HEAD
-    w_out_t = attn_w[:, out_at : out_at + q_cols]
-    gains = attn_w[:, out_at + q_cols : out_at + q_cols + 2].astype(F32).T
-    gain_one_row, gain_two_row = gains[0:1], gains[1:2]
-    w_gu, w_down_t = ffn_w[:, : 2 * units], ffn_w[:, 2 * units :]
+    shard_a = jnp.concatenate([w_query, w_keyval, w_out.T, gain_cols], axis=1)
+    shard_d = w_down.T
+    shard_g = jnp.concatenate([w_gate, w_up], axis=1)
+    if n_dp != 8:
+        shard_a, shard_d, shard_g = (
+            lax.all_gather(w, "dp", axis=0, tiled=True) for w in (shard_a, shard_d, shard_g)
+        )
 
     turn = t ^ jnp.arange(4, dtype=jnp.int32)
     positions = positions_of(segment_ids).reshape(4, quarter)[turn].reshape(length)
@@ -444,43 +700,27 @@
     valid3 = valid.reshape(length // BLK, 1, BLK)
     t1 = t.reshape(1)
 
-    parts = gather4(tokens)
-    normed, q, k, v = project(parts, gain_one_row, attn_w, cos, sin, q_cols)
+    (w_a, w_down_t, w_gu, gains, normed, q, k, v, mixed, lse, residual, n2, go_all, gh) = front(
+        n_dp, tokens, grad_output, shard_a, shard_d, shard_g, pos3, valid3, cos, sin, q_cols
+    )
+    kv_at = q_cols + 2 * HEAD
+    w_out_t = w_a[:, kv_at : kv_at + q_cols]
+    gain_one_row, gain_two_row = gains[0:1], gains[1:2]
+    x_rows = tokens.astype(F32)
+    scale_two = lax.rsqrt(jnp.mean(residual * residual, axis=-1, keepdims=True) + EPS)
     half = length // 2
-    mixed_far, lse_far = attention_forward(t1, q, k, v, pos3, valid3, half, half)
-    mixed_near, lse_near = attention_forward(t1, q, k, v, pos3, valid3, 0, half)
-    attn_far = dot_nt(mixed_far, w_out_t).astype(BF16)
-    attn_near = dot_nt(mixed_near, w_out_t).astype(BF16)
-    x_rows = tokens.astype(F32)
-    residual = x_rows + reduce4(attn_near, attn_far)
-
-    go = grad_output.astype(BF16)
-    go, _ = lax.optimization_barrier((go, parts[2]))
-    go_parts = gather4(go)
-    go_near = jnp.concatenate(go_parts[:2])
-    go_far = jnp.concatenate(go_parts[2:])
-    gh_near = dot(go_near, w_down_t)
-    gh_far = dot(go_far, w_down_t)
-
-    scale_two = lax.rsqrt(jnp.mean(residual * residual, axis=-1, keepdims=True) + EPS)
-    n2 = gather4((residual * scale_two * gain_two_row).astype(BF16))
-    n2_near = jnp.concatenate(n2[:2])
-    n2_far = jnp.concatenate(n2[2:])
-    hidden_near, dgu_near = ffn_middle(n2_near, ffn_w, gh_near)
-    hidden_far, dgu_far = ffn_middle(n2_far, ffn_w, gh_far)
-    dn2_far = dot_nt(dgu_far, w_gu).astype(BF16)
-    dn2_near = dot_nt(dgu_near, w_gu).astype(BF16)
+
+    hidden, dgu = ffn_middle(n2, w_gu, gh, half, half, ())
+    dn2_far = dot_nt(dgu[half:], w_gu).astype(BF16)
+    hidden, dgu = ffn_middle(n2, w_gu, gh, 0, half, (hidden, dgu))
+    dn2_near = dot_nt(dgu[:half], w_gu).astype(BF16)
     grad_n2 = reduce4(dn2_near, dn2_far)
 
-    ffn_far = dot_nt(hidden_far, w_down_t).astype(BF16)
-    ffn_near = dot_nt(hidden_near, w_down_t).astype(BF16)
+    ffn_far = dot_nt(hidden[half:], w_down_t).astype(BF16)
+    ffn_near = dot_nt(hidden[:half], w_down_t).astype(BF16)
     output = (residual + reduce4(ffn_near, ffn_far)).astype(BF16)
 
-    dgu = jnp.concatenate([dgu_near, dgu_far])
-    n2_all = jnp.concatenate([n2_near, n2_far])
-    hidden = jnp.concatenate([hidden_near, hidden_far])
-    go_all = jnp.concatenate([go_near, go_far])
-    grad_w_gu = dot_tn(n2_all, dgu).astype(BF16)
+    grad_w_gu = dot_tn(n2, dgu).astype(BF16)
     grad_w_down_t = dot_tn(go_all, hidden).astype(BF16)
 
     weighted = grad_n2 * gain_two_row
@@ -490,11 +730,9 @@
 
     ga = jnp.concatenate(gather4(grad_residual.astype(BF16)))
     grad_mixed = (dot(ga, w_out_t) * valid[:, None]).astype(BF16)
-    mixed = jnp.concatenate([mixed_near, mixed_far])
-    lse = jnp.concatenate([lse_near, lse_far])
     dq, dkv = attention_backward(t1, q, grad_mixed, mixed, lse, k, v, pos3, cos, sin)
     dqkv = jnp.concatenate([dq, dkv], axis=1)
-    w_qkv = attn_w[:, :out_at]
+    w_qkv = w_a[:, :kv_at]
     dn_far = dot_nt(dqkv[half:], w_qkv).astype(BF16)
     dn_near = dot_nt(dqkv[:half], w_qkv).astype(BF16)
     grad_normed = reduce4(dn_near, dn_far)

time: 587 us -> 552 us (0.940)
  Pallas kernels: 84.7 us -> 222 us
  waiting for transfers between devices: 209 us -> 112 us
  matrix products: 112 us -> 83.3 us
  starting transfers between devices: 65.4 us -> 41 us
  local copies, waits for them, and re-layouts: 51.2 us -> 27.8 us
    pallas_call x5 -> x3, Pallas kernels: 58.8 us -> 196 us  [the longest x1 166 us: front(): pl.pallas_call(functools.partial(front_kernel, n_dp), in_specs=[vmem, hbm...]
    ppermute x14 -> x0, waiting for transfers between devices: 85.5 us -> none  [the longest x8 84.3 us: dp_gather(): ahead = lax.ppermute(ahead, 'dp', forth)]
    dot_general x3 -> x1, matrix products: 24.9 us -> 6.24 us  [dot(): return jnp.dot(left, right, preferred_element_type=F32)]
    ppermute x14 -> x0, starting transfers between devices: 16.9 us -> none  [the longest x8 14.5 us: dp_gather(): ahead = lax.ppermute(ahead, 'dp', forth)]
    dynamic_update_slice x15 -> x0, local copies, waits for them, and re-layouts: 16 us -> none  [put(): return lax.dynamic_update_slice_in_dim(full, block, table[me] * rows, 0)]
    ppermute x5, waiting for transfers between devices: 0.16 us -> 14.8 us  [dp_scatter(): ahead = lax.ppermute(part(far), 'dp', forth)]
    ppermute x9 -> x5, waiting for transfers between devices: 87 us -> 75.3 us  [across(): return lax.ppermute(v, 'tensor', [(i, i ^ 2) for i in range(4)])]
    ppermute x15, waiting for transfers between devices: 15.3 us -> 4.45 us  [dp_scatter(): ahead = lax.ppermute(ahead + part(far - s), 'dp', forth)]
  transfers between devices with their start and end apart: 75 -> 49, of which waited for: 21 -> 14; matrix products, arithmetic and copies ran while one was open for 35% -> 24% of each run, Pallas kernels for 15% -> 8%
where the time goes in v2:
time: 552 us; the launch traced here: 545 us
  Pallas kernels  222 us (40%)
  waiting for transfers between devices  112 us (20%)
  matrix products  83.3 us (15%)
  other arithmetic  52.6 us (10%)
  starting transfers between devices  41 us (7%)
  local copies, waits for them, and re-layouts  27.8 us (5%)
  between operations  6.68 us (1%)
    pallas_call x1, Pallas kernels, front(): pl.pallas_call(functools.partial(front_kernel, n_dp), in_specs=[vmem, hbm...  166 us
    ppermute x5, waiting for transfers between devices, across(): return lax.ppermute(v, 'tensor', [(i, i ^ 2) for i in range(4)])  75.3 us
    dot_general x4, matrix products, dot_tn(): return lax.dot_general(left, right, TN, preferred_element_type=F32)  43.3 us
    dot_general x6, matrix products, dot_nt(): return lax.dot_general(left, right, NT, preferred_element_type=F32)  33.7 us
    pallas_call x2, Pallas kernels, ffn_middle(): pl.pallas_call(body, grid=(rows // BLK,), in_specs=[row_spec(width), pl.B...  29.8 us
    pallas_call x1, Pallas kernels, attention_backward(): pl.pallas_call(attn_bwd_kernel, grid_spec=pltpu.PrefetchScalarGridSpec(nu...  25.8 us
    add x15, other arithmetic, dp_scatter(): ahead = lax.ppermute(ahead + part(far - s), 'dp', forth)  18.4 us
    ppermute x15, starting transfers between devices, dp_scatter(): ahead = lax.ppermute(ahead + part(far - s), 'dp', forth)  16.1 us
  transfers between devices with their start and end apart: 49, of which 14 were waited for; matrix products, arithmetic and copies ran while one was open for 24% of the time, Pallas kernels for 8%

profile of v2, /device:TPU:0, one launch (start us, length us, event | category | flops | bytes accessed | tf_op | source)
XLA Modules:
  0.0 545.1 jit_solution(15177868980284917415)
XLA Ops:
  8.3 3.7 fusion.24
  14.8 166.2 %front.1 = (bf16[1536,1152]{1,0:T(8,128)(2,1)}, bf16[1536,1152]{1,0:T(8,128)(2,1)}, bf16[1536,2304]{1,0:T(8,128)(2,1)}, f32[8,1536]{1,0:T(8,128)}, bf16[2048,153...) custom-call(bf16[512,1536]{1,0:T(8,128)(2,1)} %tokens.1, ...), custom_call_target="tpu_custom_call" | custom-call | flops 14495514624 | bytes 67108864 | tf_op jit(solution)/shard_map/front/pallas_call | solution.py:422
  181.0 14.4 %ffn_middle.2 = (bf16[2048,1152]{1,0:T(8,128)(2,1)}, bf16[2048,2304]{1,0:T(8,128)(2,1)}) custom-call(bf16[2048,1536]{1,0:T(8,128)(2,1)} %get-tuple-element.30.n_ref, bf16[1536,2304]{1,0:T(8,128)(2,1)} %get-tuple-element.31.w_ref, bf16[2048,1152]{1,0:T(8,128)(2,1)} %get-tuple-element.32.gh_ref), custom_call_target="tpu_custom_call" | custom-call | flops 7247757312 | bytes 22020096 | tf_op jit(solution)/shard_map/ffn_middle/pallas_call | solution.py:590
  195.4 9.4 %fusion.7 = bf16[1024,1536]{1,0:T(8,128)(2,1)S(1)} fusion(bf16[1536,2304]{1,0:T(8,128)(2,1)S(1)} %copy-done.15, bf16[2048,2304]{1,0:T(8,128)(2,1)} %get-tuple-element.34.refs_1_), kind=kOutput, calls=%fused_computation.16 | convolution fusion | flops 7249330176 | bytes 14942208 | tf_op jit(solution)/shard_map/dot_general | solution.py:29
  207.8 15.4 %ffn_middle.3 = (bf16[2048,1152]{1,0:T(8,128)(2,1)}, bf16[2048,2304]{1,0:T(8,128)(2,1)}) custom-call(bf16[2048,1536]{1,0:T(8,128)(2,1)} %get-tuple-element.30.n_ref, bf16[1536,2304]{1,0:T(8,128)(2,1)} %get-tuple-element.31.w_ref, bf16[2048,1152]{1,0:T(8,128)(2,1)} %get-tuple-element.32.gh_ref, ...), custom_call_target="tpu_custom_call", output_to_operand_aliasing={{0}: (3, {}), {1}: (4, {})} | custom-call | flops 7247757312 | bytes 22020096 | tf_op jit(solution)/shard_map/ffn_middle/pallas_call | solution.py:590
  223.3 9.5 %fusion.4 = bf16[1024,1536]{1,0:T(8,128)(2,1)S(1)} fusion(bf16[1536,2304]{1,0:T(8,128)(2,1)S(1)} %bitcast.46, bf16[2048,2304]{1,0:T(8,128)(2,1)} %get-tuple-element.37), kind=kOutput, calls=%fused_computation.15 | convolution fusion | flops 7249330176 | bytes 14942208 | tf_op jit(solution)/shard_map/dot_general | solution.py:29
  234.3 4.5 convolution_convert_fusion.4
  241.4 4.5 convolution_convert_fusion.5
  250.2 11.9 %convolution_convert_fusion.1 = bf16[1536,1152]{1,0:T(8,128)(2,1)S(1)} fusion(bf16[2048,1536]{1,0:T(8,128)(2,1)} %get-tuple-element.48, bf16[2048,1152]{1,0:T(8,128)(2,1)} %get-tuple-element.35), kind=kOutput, calls=%fused_computation.3 | convolution fusion | flops 7249526784 | bytes 14548992 | tf_op jit(solution)/shard_map/dot_general | solution.py:33
  266.4 20.8 %convolution_convert_fusion = bf16[1536,2304]{1,0:T(8,128)(2,1)} fusion(bf16[2048,1536]{1,0:T(8,128)(2,1)} %get-tuple-element.30.n_ref, bf16[2048,2304]{1,0:T(8,128)(2,1)} %get-tuple-element.37), kind=kOutput, calls=%fused_computation.2 | convolution fusion | flops 14499053568 | bytes 22806528 | tf_op jit(solution)/shard_map/dot_general | solution.py:33
  302.5 14.8 %collective-permute-done.35 = bf16[192,2304]{1,0:T(8,128)(2,1)S(1)} collective-permute-done((bf16[192,2304]{1,0:T(8,128)(2,1)S(1)}, bf16[192,2304]{1,0:T(8,128)(2,1)S(1)}, u32[]{:S(2)}, u32[]{:S(2)}) %collective-permute-start.35) | collective-permute-done | bytes 884768 | tf_op jit(solution)/shard_map/ppermute | solution.py:637
  318.1 3.0 dynamic-slice_add_fusion.4
  321.1 7.6 %collective-permute-done.46 = bf16[192,1152]{1,0:T(8,128)(2,1)S(1)} collective-permute-done((bf16[192,1152]{1,0:T(8,128)(2,1)S(1)}, bf16[192,1152]{1,0:T(8,128)(2,1)S(1)}, u32[]{:S(2)}, u32[]{:S(2)}) %collective-permute-start.46) | collective-permute-done | bytes 442400 | tf_op jit(solution)/shard_map/ppermute | solution.py:638
  331.8 6.1 %collective-permute-done.5 = bf16[512,1536]{1,0:T(8,128)(2,1)S(1)} collective-permute-done((bf16[512,1536]{1,0:T(8,128)(2,1)S(1)}, bf16[512,1536]{1,0:T(8,128)(2,1)S(1)}, u32[]{:S(2)}, u32[]{:S(2)}) %collective-permute-start.5) | collective-permute-done | bytes 1572896 | tf_op jit(solution)/shard_map/ppermute | solution.py:669
  338.8 2.8 multiply_reduce_fusion
  343.0 27.3 %collective-permute-done.2 = bf16[512,1536]{1,0:T(8,128)(2,1)S(1)} collective-permute-done((bf16[512,1536]{1,0:T(8,128)(2,1)S(1)}, bf16[512,1536]{1,0:T(8,128)(2,1)S(1)}, u32[]{:S(2)}, u32[]{:S(2)}) %collective-permute-start.2) | collective-permute-done | bytes 1572896 | tf_op jit(solution)/shard_map/ppermute | solution.py:669
  370.3 5.3 fusion.37
  378.4 2.4 dynamic-slice_add_fusion.7
  382.8 3.3 dynamic-slice_add_fusion.3
  388.3 5.7 %collective-permute-done.48 = bf16[192,1152]{1,0:T(8,128)(2,1)} collective-permute-done((bf16[192,1152]{1,0:T(8,128)(2,1)S(1)}, bf16[192,1152]{1,0:T(8,128)(2,1)}, u32[]{:S(2)}, u32[]{:S(2)}) %collective-permute-start.48) | collective-permute-done | bytes 442400 | tf_op jit(solution)/shard_map/ppermute | solution.py:642
  394.0 16.9 %collective-permute-done.7 = bf16[512,1536]{1,0:T(8,128)(2,1)} collective-permute-done((bf16[512,1536]{1,0:T(8,128)(2,1)}, bf16[512,1536]{1,0:T(8,128)(2,1)}, u32[]{:S(2)}, u32[]{:S(2)}) %collective-permute-start.7) | collective-permute-done | bytes 1572896 | tf_op jit(solution)/shard_map/ppermute | solution.py:669
  411.4 2.3 add_bitcast_fusion
  418.2 6.2 %multiply_convert_fusion.do = bf16[2048,384]{1,0:T(8,128)(2,1)S(1)} fusion(f32[2048]{0:T(1024)S(1)} %bitcast.51, bf16[1536,1152]{1,0:T(8,128)(2,1)S(1)} %copy-done.46, bf16[512,1536]{1,0:T(8,128)(2,1)} %collective-permute-done.8, bf16[512,1536]{1,0:T(8,128)(2,1)} %collective-permute-done.7, bf16[512,1536]{1,0:T(8,128)(2,1)} %collective-permute-done.6, ...), kind=kOutput, calls=%fused_computation.28 | convolution fusion | flops 2442657792 | bytes 9052160 | tf_op jit(solution)/shard_map/dot_general | solution.py:25
  424.5 25.8 %attention_backward.1 = (bf16[2048,384]{1,0:T(8,128)(2,1)S(1)}, bf16[2048,256]{1,0:T(8,128)(2,1)S(1)}) custom-call(s32[1]{0:T(128)} %bitcast.5.t_ref, bf16[2048,384]{1,0:T(8,128)(2,1)S(1)} %copy-done.4, bf16[2048,384]{1,0:T(8,128)(2,1)S(1)} %multiply_convert_fusion.do, bf16[2048,384]{1,0:T(8,128)(2,1)S(1)} %copy-done.3, f32[8,1,768]{2,1,0:T(1,128)S(1)} %copy-done.7, ...), custom_call_target="tpu_custom_call" | custom-call | flops 16106127360 | bytes 9437184 | tf_op jit(solution)/shard_map/attention_backward/pallas_call | solution.py:530
  450.5 2.9 convolution_convert_fusion.2
  456.7 2.9 convolution_convert_fusion.3
  461.3 5.1 convolution_convert_fusion.6
  468.2 5.5 %convolution_convert_fusion.7 = bf16[1536,384]{1,0:T(8,128)(2,1)S(1)} fusion(bf16[2048,384]{1,0:T(8,128)(2,1)S(1)} %copy-done.3, bf16[512,1536]{1,0:T(8,128)(2,1)} %collective-permute-done.8, bf16[512,1536]{1,0:T(8,128)(2,1)} %collective-permute-done.7, bf16[512,1536]{1,0:T(8,128)(2,1)} %collective-permute-done.6, bf16[512,1536]{1,0:T(8,128)(2,1)} %get-tuple-element.82), kind=kOutput, calls=%fused_computation.36 | convolution fusion | flops 2441674752 | bytes 9043968 | tf_op jit(solution)/shard_map/dot_general | solution.py:33
  478.0 19.1 %collective-permute-done.11 = bf16[512,1536]{1,0:T(8,128)(2,1)S(1)} collective-permute-done((bf16[512,1536]{1,0:T(8,128)(2,1)S(1)}, bf16[512,1536]{1,0:T(8,128)(2,1)S(1)}, u32[]{:S(2)}, u32[]{:S(2)}) %collective-permute-start.11) | collective-permute-done | bytes 1572896 | tf_op jit(solution)/shard_map/ppermute | solution.py:669
  513.7 2.6 collective-permute-done.21
  534.5 2.8 fusion.12
  537.4 5.9 %collective-permute-done.27 = f32[192,384]{1,0:T(8,128)S(1)} collective-permute-done((f32[192,384]{1,0:T(8,128)S(1)}, f32[192,384]{1,0:T(8,128)S(1)}, u32[]{:S(2)}, u32[]{:S(2)}) %collective-permute-start.27) | collective-permute-done | bytes 294944 | tf_op jit(solution)/shard_map/ppermute | solution.py:669
  (283 shorter events, 101.5 us)
Async XLA Ops:
  207.7 89.8 %collective-permute-start.4 = (bf16[512,1536]{1,0:T(8,128)(2,1)}, bf16[512,1536]{1,0:T(8,128)(2,1)}, u32[]{:S(2)}, u32[]{:S(2)}) collective-permute-start(bf16[512,1536]{1,0:T(8,128)(2,1)} %slice.138), channel_id=1, source_target_pairs={{0,1},{1,0},{2,3},{3,2},{4,5},{5,4},{6,7},{7,6},{8,9},{9,8},{10,11... | collective-permute-start | bytes 4718600 | tf_op jit(solution)/shard_map/ppermute | solution.py:666
  234.2 96.7 %collective-permute-start.3 = (bf16[512,1536]{1,0:T(8,128)(2,1)}, bf16[512,1536]{1,0:T(8,128)(2,1)}, u32[]{:S(2)}, u32[]{:S(2)}) collective-permute-start(bf16[512,1536]{1,0:T(8,128)(2,1)} %slice.136), channel_id=1, source_target_pairs={{0,1},{1,0},{2,3},{3,2},{4,5},{5,4},{6,7},{7,6},{8,9},{9,8},{10,11... | collective-permute-start | bytes 4718600 | tf_op jit(solution)/shard_map/ppermute | solution.py:666
  241.0 59.6 %collective-permute-start.1 = (bf16[512,1536]{1,0:T(8,128)(2,1)}, bf16[512,1536]{1,0:T(8,128)(2,1)}, u32[]{:S(2)}, u32[]{:S(2)}) collective-permute-start(bf16[512,1536]{1,0:T(8,128)(2,1)} %slice.134), channel_id=1, source_target_pairs={{0,1},{1,0},{2,3},{3,2},{4,5},{5,4},{6,7},{7,6},{8,9},{9,8},{10,11... | collective-permute-start | bytes 4718600 | tf_op jit(solution)/shard_map/ppermute | solution.py:666
  248.9 92.8 %collective-permute-start = (bf16[512,1536]{1,0:T(8,128)(2,1)}, bf16[512,1536]{1,0:T(8,128)(2,1)}, u32[]{:S(2)}, u32[]{:S(2)}) collective-permute-start(bf16[512,1536]{1,0:T(8,128)(2,1)} %slice.132), channel_id=1, source_target_pairs={{0,1},{1,0},{2,3},{3,2},{4,5},{5,4},{6,7},{7,6},{8,9},{9,8},{10,11... | collective-permute-start | bytes 4718600 | tf_op jit(solution)/shard_map/ppermute | solution.py:666
  264.9 30.6 %collective-permute-start.42 = (bf16[192,1152]{1,0:T(8,128)(2,1)}, bf16[192,1152]{1,0:T(8,128)(2,1)}, u32[]{:S(2)}, u32[]{:S(2)}) collective-permute-start(bf16[192,1152]{1,0:T(8,128)(2,1)} %constant_dynamic-slice_fusion.1), channel_id=1, source_target_pairs={{4,12},{12,20},{20,28},{28,24},{24,16},{16,8},{8,0},{0,4},{5,13},{... | collective-permute-start | bytes 1327112 | tf_op jit(solution)/shard_map/ppermute | solution.py:637
  295.5 21.8 %collective-permute-start.35 = (bf16[192,2304]{1,0:T(8,128)(2,1)S(1)}, bf16[192,2304]{1,0:T(8,128)(2,1)S(1)}, u32[]{:S(2)}, u32[]{:S(2)}) collective-permute-start(bf16[192,2304]{1,0:T(8,128)(2,1)S(1)} %constant_dynamic-slice_fusion.3), channel_id=1, source_target_pairs={{0,8},{8,16},{16,24},{24,28},{28,20},{20,12},{12,4},{4,0},{1,9},{9... | collective-permute-start | bytes 2654216 | tf_op jit(solution)/shard_map/ppermute | solution.py:637
  297.5 20.5 %collective-permute-start.43 = (bf16[192,1152]{1,0:T(8,128)(2,1)S(1)}, bf16[192,1152]{1,0:T(8,128)(2,1)S(1)}, u32[]{:S(2)}, u32[]{:S(2)}) collective-permute-start(bf16[192,1152]{1,0:T(8,128)(2,1)S(1)} %get-tuple-element.94), channel_id=1, source_target_pairs={{4,12},{12,20},{20,28},{28,24},{24,16},{16,8},{8,0},{0,4},{5,13},{... | collective-permute-start | bytes 1327112 | tf_op jit(solution)/shard_map/ppermute | solution.py:640
  300.6 37.4 %collective-permute-start.5 = (bf16[512,1536]{1,0:T(8,128)(2,1)S(1)}, bf16[512,1536]{1,0:T(8,128)(2,1)S(1)}, u32[]{:S(2)}, u32[]{:S(2)}) collective-permute-start(bf16[512,1536]{1,0:T(8,128)(2,1)S(1)} %add_convert_fusion.1), channel_id=1, source_target_pairs={{0,2},{1,3},{2,0},{3,1},{4,6},{5,7},{6,4},{7,5},{8,10},{9,11},{10,... | collective-permute-start | bytes 4718600 | tf_op jit(solution)/shard_map/ppermute | solution.py:669
  317.3 11.4 %collective-permute-start.46 = (bf16[192,1152]{1,0:T(8,128)(2,1)S(1)}, bf16[192,1152]{1,0:T(8,128)(2,1)S(1)}, u32[]{:S(2)}, u32[]{:S(2)}) collective-permute-start(bf16[192,1152]{1,0:T(8,128)(2,1)S(1)} %get-tuple-element.95), channel_id=1, source_target_pairs={{12,4},{20,12},{28,20},{24,28},{16,24},{8,16},{0,8},{4,0},{13,5},{... | collective-permute-start | bytes 1327112 | tf_op jit(solution)/shard_map/ppermute | solution.py:638
  318.1 52.2 %collective-permute-start.2 = (bf16[512,1536]{1,0:T(8,128)(2,1)S(1)}, bf16[512,1536]{1,0:T(8,128)(2,1)S(1)}, u32[]{:S(2)}, u32[]{:S(2)}) collective-permute-start(bf16[512,1536]{1,0:T(8,128)(2,1)S(1)} %add_convert_fusion.3), channel_id=1, source_target_pairs={{0,2},{1,3},{2,0},{3,1},{4,6},{5,7},{6,4},{7,5},{8,10},{9,11},{10,... | collective-permute-start | bytes 4718600 | tf_op jit(solution)/shard_map/ppermute | solution.py:669
  328.7 54.2 %collective-permute-start.36 = (bf16[192,2304]{1,0:T(8,128)(2,1)}, bf16[192,2304]{1,0:T(8,128)(2,1)}, u32[]{:S(2)}, u32[]{:S(2)}) collective-permute-start(bf16[192,2304]{1,0:T(8,128)(2,1)} %get-tuple-element.88), channel_id=1, source_target_pairs={{0,8},{8,16},{16,24},{24,28},{28,20},{20,12},{12,4},{4,0},{1,9},{9... | collective-permute-start | bytes 2654216 | tf_op jit(solution)/shard_map/ppermute | solution.py:640
  330.9 51.9 %collective-permute-start.39 = (bf16[192,2304]{1,0:T(8,128)(2,1)}, bf16[192,2304]{1,0:T(8,128)(2,1)}, u32[]{:S(2)}, u32[]{:S(2)}) collective-permute-start(bf16[192,2304]{1,0:T(8,128)(2,1)} %get-tuple-element.89), channel_id=1, source_target_pairs={{8,0},{16,8},{24,16},{28,24},{20,28},{12,20},{4,12},{0,4},{9,1},{1... | collective-permute-start | bytes 2654216 | tf_op jit(solution)/shard_map/ppermute | solution.py:638
  338.0 40.4 %collective-permute-start.44 = (bf16[192,1152]{1,0:T(8,128)(2,1)}, bf16[192,1152]{1,0:T(8,128)(2,1)}, u32[]{:S(2)}, u32[]{:S(2)}) collective-permute-start(bf16[192,1152]{1,0:T(8,128)(2,1)} %get-tuple-element.92), channel_id=1, source_target_pairs={{4,12},{12,20},{20,28},{28,24},{24,16},{16,8},{8,0},{0,4},{5,13},{... | collective-permute-start | bytes 1327112 | tf_op jit(solution)/shard_map/ppermute | solution.py:640
  341.7 36.7 %collective-permute-start.47 = (bf16[192,1152]{1,0:T(8,128)(2,1)}, bf16[192,1152]{1,0:T(8,128)(2,1)}, u32[]{:S(2)}, u32[]{:S(2)}) collective-permute-start(bf16[192,1152]{1,0:T(8,128)(2,1)} %get-tuple-element.93), channel_id=1, source_target_pairs={{12,4},{20,12},{28,20},{24,28},{16,24},{8,16},{0,8},{4,0},{13,5},{... | collective-permute-start | bytes 1327112 | tf_op jit(solution)/shard_map/ppermute | solution.py:642
  375.6 35.3 %collective-permute-start.7 = (bf16[512,1536]{1,0:T(8,128)(2,1)}, bf16[512,1536]{1,0:T(8,128)(2,1)}, u32[]{:S(2)}, u32[]{:S(2)}) collective-permute-start(bf16[512,1536]{1,0:T(8,128)(2,1)} %get-tuple-element.82), channel_id=1, source_target_pairs={{0,2},{1,3},{2,0},{3,1},{4,6},{5,7},{6,4},{7,5},{8,10},{9,11},{10,... | collective-permute-start | bytes 4718600 | tf_op jit(solution)/shard_map/ppermute | solution.py:669
  380.8 13.2 %collective-permute-start.48 = (bf16[192,1152]{1,0:T(8,128)(2,1)S(1)}, bf16[192,1152]{1,0:T(8,128)(2,1)}, u32[]{:S(2)}, u32[]{:S(2)}) collective-permute-start(bf16[192,1152]{1,0:T(8,128)(2,1)S(1)} %get-tuple-element.91), channel_id=1, source_target_pairs={{12,4},{20,12},{28,20},{24,28},{16,24},{8,16},{0,8},{4,0},{13,5},{... | collective-permute-start | bytes 1327112 | tf_op jit(solution)/shard_map/ppermute | solution.py:642
  381.9 29.4 %collective-permute-start.45 = (bf16[192,1152]{1,0:T(8,128)(2,1)}, bf16[192,1152]{1,0:T(8,128)(2,1)}, u32[]{:S(2)}, u32[]{:S(2)}) collective-permute-start(bf16[192,1152]{1,0:T(8,128)(2,1)} %get-tuple-element.90), channel_id=1, source_target_pairs={{4,12},{12,20},{20,28},{28,24},{24,16},{16,8},{8,0},{0,4},{5,13},{... | collective-permute-start | bytes 1327112 | tf_op jit(solution)/shard_map/ppermute | solution.py:640
  386.1 27.6 %collective-permute-start.37 = (bf16[192,2304]{1,0:T(8,128)(2,1)}, bf16[192,2304]{1,0:T(8,128)(2,1)S(1)}, u32[]{:S(2)}, u32[]{:S(2)}) collective-permute-start(bf16[192,2304]{1,0:T(8,128)(2,1)} %get-tuple-element.86), channel_id=1, source_target_pairs={{0,8},{8,16},{16,24},{24,28},{28,20},{20,12},{12,4},{4,0},{1,9},{9... | collective-permute-start | bytes 2654216 | tf_op jit(solution)/shard_map/ppermute | solution.py:640
  387.2 26.5 %collective-permute-start.40 = (bf16[192,2304]{1,0:T(8,128)(2,1)S(1)}, bf16[192,2304]{1,0:T(8,128)(2,1)}, u32[]{:S(2)}, u32[]{:S(2)}) collective-permute-start(bf16[192,2304]{1,0:T(8,128)(2,1)S(1)} %get-tuple-element.87), channel_id=1, source_target_pairs={{8,0},{16,8},{24,16},{28,24},{20,28},{12,20},{4,12},{0,4},{9,1},{1... | collective-permute-start | bytes 2654216 | tf_op jit(solution)/shard_map/ppermute | solution.py:642
  394.0 24.0 %collective-permute-start.6 = (bf16[512,1536]{1,0:T(8,128)(2,1)}, bf16[512,1536]{1,0:T(8,128)(2,1)}, u32[]{:S(2)}, u32[]{:S(2)}) collective-permute-start(bf16[512,1536]{1,0:T(8,128)(2,1)} %get-tuple-element.82), channel_id=1, source_target_pairs={{0,1},{1,0},{2,3},{3,2},{4,5},{5,4},{6,7},{7,6},{8,9},{9,8},{10,11... | collective-permute-start | bytes 4718600 | tf_op jit(solution)/shard_map/ppermute | solution.py:666
  416.0 37.7 %collective-permute-start.41 = (bf16[192,2304]{1,0:T(8,128)(2,1)S(1)}, bf16[192,2304]{1,0:T(8,128)(2,1)S(1)}, u32[]{:S(2)}, u32[]{:S(2)}) collective-permute-start(bf16[192,2304]{1,0:T(8,128)(2,1)S(1)} %get-tuple-element.85), channel_id=1, source_target_pairs={{8,0},{16,8},{24,16},{28,24},{20,28},{12,20},{4,12},{0,4},{9,1},{1... | collective-permute-start | bytes 2654216 | tf_op jit(solution)/shard_map/ppermute | solution.py:642
  416.4 37.3 %collective-permute-start.38 = (bf16[192,2304]{1,0:T(8,128)(2,1)S(1)}, bf16[192,2304]{1,0:T(8,128)(2,1)S(1)}, u32[]{:S(2)}, u32[]{:S(2)}) collective-permute-start(bf16[192,2304]{1,0:T(8,128)(2,1)S(1)} %get-tuple-element.84), channel_id=1, source_target_pairs={{0,8},{8,16},{16,24},{24,28},{28,20},{20,12},{12,4},{4,0},{1,9},{9... | collective-permute-start | bytes 2654216 | tf_op jit(solution)/shard_map/ppermute | solution.py:640
  459.7 18.2 %collective-permute-start.9 = (bf16[512,1536]{1,0:T(8,128)(2,1)S(1)}, bf16[512,1536]{1,0:T(8,128)(2,1)S(1)}, u32[]{:S(2)}, u32[]{:S(2)}) collective-permute-start(bf16[512,1536]{1,0:T(8,128)(2,1)S(1)} %slice.141), channel_id=1, source_target_pairs={{0,1},{1,0},{2,3},{3,2},{4,5},{5,4},{6,7},{7,6},{8,9},{9,8},{10,11... | collective-permute-start | bytes 4718600 | tf_op jit(solution)/shard_map/ppermute | solution.py:666
  460.7 36.4 %collective-permute-start.11 = (bf16[512,1536]{1,0:T(8,128)(2,1)S(1)}, bf16[512,1536]{1,0:T(8,128)(2,1)S(1)}, u32[]{:S(2)}, u32[]{:S(2)}) collective-permute-start(bf16[512,1536]{1,0:T(8,128)(2,1)S(1)} %add_convert_fusion), channel_id=1, source_target_pairs={{0,2},{1,3},{2,0},{3,1},{4,6},{5,7},{6,4},{7,5},{8,10},{9,11},{10,... | collective-permute-start | bytes 4718600 | tf_op jit(solution)/shard_map/ppermute | solution.py:669
  474.5 26.5 %collective-permute-start.28 = (bf16[192,384]{1,0:T(8,128)(2,1)}, bf16[192,384]{1,0:T(8,128)(2,1)}, u32[]{:S(2)}, u32[]{:S(2)}) collective-permute-start(bf16[192,384]{1,0:T(8,128)(2,1)} %constant_dynamic-slice_fusion.2), channel_id=1, source_target_pairs={{4,12},{12,20},{20,28},{28,24},{24,16},{16,8},{8,0},{0,4},{5,13},{... | collective-permute-start | bytes 442376 | tf_op jit(solution)/shard_map/ppermute | solution.py:637
  475.9 29.2 %collective-permute-start.13 = (bf16[192,640]{1,0:T(8,128)(2,1)}, bf16[192,640]{1,0:T(8,128)(2,1)}, u32[]{:S(2)}, u32[]{:S(2)}) collective-permute-start(bf16[192,640]{1,0:T(8,128)(2,1)} %get-tuple-element.101), channel_id=1, source_target_pairs={{0,8},{8,16},{16,24},{24,28},{28,20},{20,12},{12,4},{4,0},{1,9},{9... | collective-permute-start | bytes 737288 | tf_op jit(solution)/shard_map/ppermute | solution.py:640
  477.4 27.8 %collective-permute-start.16 = (bf16[192,640]{1,0:T(8,128)(2,1)}, bf16[192,640]{1,0:T(8,128)(2,1)}, u32[]{:S(2)}, u32[]{:S(2)}) collective-permute-start(bf16[192,640]{1,0:T(8,128)(2,1)} %get-tuple-element.102), channel_id=1, source_target_pairs={{8,0},{16,8},{24,16},{28,24},{20,28},{12,20},{4,12},{0,4},{9,1},{1... | collective-permute-start | bytes 737288 | tf_op jit(solution)/shard_map/ppermute | solution.py:638
  506.5 10.6 %collective-permute-start.14 = (bf16[192,640]{1,0:T(8,128)(2,1)S(1)}, bf16[192,640]{1,0:T(8,128)(2,1)S(1)}, u32[]{:S(2)}, u32[]{:S(2)}) collective-permute-start(bf16[192,640]{1,0:T(8,128)(2,1)S(1)} %get-tuple-element.99), channel_id=1, source_target_pairs={{0,8},{8,16},{16,24},{24,28},{28,20},{20,12},{12,4},{4,0},{1,9},{9... | collective-permute-start | bytes 737288 | tf_op jit(solution)/shard_map/ppermute | solution.py:640
  507.5 9.6 %collective-permute-start.17 = (bf16[192,640]{1,0:T(8,128)(2,1)S(1)}, bf16[192,640]{1,0:T(8,128)(2,1)S(1)}, u32[]{:S(2)}, u32[]{:S(2)}) collective-permute-start(bf16[192,640]{1,0:T(8,128)(2,1)S(1)} %get-tuple-element.100), channel_id=1, source_target_pairs={{8,0},{16,8},{24,16},{28,24},{20,28},{12,20},{4,12},{0,4},{9,1},{1... | collective-permute-start | bytes 737288 | tf_op jit(solution)/shard_map/ppermute | solution.py:642
  511.7 10.8 %collective-permute-start.30 = (bf16[192,384]{1,0:T(8,128)(2,1)S(1)}, bf16[192,384]{1,0:T(8,128)(2,1)S(1)}, u32[]{:S(2)}, u32[]{:S(2)}) collective-permute-start(bf16[192,384]{1,0:T(8,128)(2,1)S(1)} %get-tuple-element.107), channel_id=1, source_target_pairs={{4,12},{12,20},{20,28},{28,24},{24,16},{16,8},{8,0},{0,4},{5,13},{... | collective-permute-start | bytes 442376 | tf_op jit(solution)/shard_map/ppermute | solution.py:640
  511.8 10.6 %collective-permute-start.33 = (bf16[192,384]{1,0:T(8,128)(2,1)S(1)}, bf16[192,384]{1,0:T(8,128)(2,1)S(1)}, u32[]{:S(2)}, u32[]{:S(2)}) collective-permute-start(bf16[192,384]{1,0:T(8,128)(2,1)S(1)} %get-tuple-element.108), channel_id=1, source_target_pairs={{12,4},{20,12},{28,20},{24,28},{16,24},{8,16},{0,8},{4,0},{13,5},{... | collective-permute-start | bytes 442376 | tf_op jit(solution)/shard_map/ppermute | solution.py:642
  522.5 9.7 %collective-permute-start.34 = (bf16[192,384]{1,0:T(8,128)(2,1)S(1)}, bf16[192,384]{1,0:T(8,128)(2,1)S(1)}, u32[]{:S(2)}, u32[]{:S(2)}) collective-permute-start(bf16[192,384]{1,0:T(8,128)(2,1)S(1)} %get-tuple-element.106), channel_id=1, source_target_pairs={{12,4},{20,12},{28,20},{24,28},{16,24},{8,16},{0,8},{4,0},{13,5},{... | collective-permute-start | bytes 442376 | tf_op jit(solution)/shard_map/ppermute | solution.py:642
  (69 other events, 858.1 us)
